TPU v7x, 256 devices: a whole 4x4x8 slice. The times are simulated.
256 devices in a mesh: dp: 2 (over core), wide: 128 (over z, x, y).
Axes of the slice: x: 4, y: 4, z: 8, core: 2. Of those that a mesh axis runs over, the one named last changes fastest.
Arguments:
- spec_cot: bfloat16 [2, 256, 256, 296], P('dp', 'wide'), may hold values from -24 to 24
- grid_state: bfloat16 [2, 512, 1024, 148], P('dp', 'wide'), may hold values from -6 to 6
- weight_in: bfloat16 [148, 256], replicated, may hold values from -0.5 to 0.5
- bias_in: float32 [256], replicated, may hold values from -4 to 4
- weight_out: bfloat16 [256, 148], replicated, may hold values from -0.375 to 0.375
- legendre: bfloat16 [256, 256, 512], P('wide'), as said below
- row_order: int32 [512], replicated, may hold values from 0 to 511, as said below
- mode_order: int32 [256], replicated, may hold values from 0 to 255, as said below
Outputs:
- spec_grad: bfloat16 [2, 256, 256, 296], P('dp', 'wide')
- grad_weight_in: float32 [148, 256], replicated
- grad_bias_in: float32 [256], replicated
- grad_weight_out: float32 [256, 148], replicated
Inputs may be any that keep to these rules, and one draw needn't show every extreme that they name: `row_order`: slot 2i holds a row j with j < 256 and slot 2i + 1 its mirror row 511 - j; every row appears once. `mode_order`: slots 2i and 2i + 1 hold wavenumbers m < 128 and 255 - m; every wavenumber appears once. legendre[k, l, r] is the associated Legendre function of degree l and order mode_order[k], normalized to unit square integral over [-1, 1] without the Condon-Shortley phase, at x = cos(theta) of the row row_order[r] (theta as in the first step, x negative on the southern rows), zero for l below the order; mirror rows differ exactly by the sign (-1)^(l + m).
All inputs are finite; a program needn't handle non-finite values.
Results may differ from a plain program's by a relative error of at most 0.011.
Values may be sent and summed in bfloat16 or wider, within the bound.
A program may use at most 64 MiB of HBM per device.

v0:
```python
import math

import jax
import jax.numpy as jnp
from jax import lax
from jax.sharding import PartitionSpec as P


def row_weights(row_order, lat_total):
    north_index = jnp.minimum(row_order, lat_total - 1 - row_order)
    colatitude = (north_index.astype(jnp.float32) + 0.5) * (math.pi / lat_total)
    return jnp.sin(colatitude) * (math.pi / lat_total)


def wave_angles(mode_order, lon_total):
    longitude = jnp.arange(lon_total, dtype=jnp.int32)
    phase_index = mode_order[:, None] * longitude[None, :] % lon_total
    return phase_index.astype(jnp.float32) * (2.0 * math.pi / lon_total)


def back_table(mode_order, lon_total):
    angles = wave_angles(mode_order, lon_total)
    return jnp.stack([jnp.cos(angles) / lon_total, -jnp.sin(angles) / lon_total], axis=1).astype(
        jnp.bfloat16
    )


def forward_table(mode_order, lon_total):
    angles = wave_angles(mode_order, lon_total)
    multiple = jnp.where(mode_order == 0, 1.0, 2.0)[:, None]
    stacked = jnp.stack([multiple * jnp.cos(angles), -multiple * jnp.sin(angles)], axis=2)
    return jnp.transpose(stacked, (1, 0, 2)).astype(jnp.bfloat16)


def per_device(
    spec_cot, grid_state, weight_in, bias_in, weight_out, legendre, row_order, mode_order
):
    samples = grid_state.shape[0]
    lat_local = grid_state.shape[1]
    lon_total = grid_state.shape[2]
    channels = grid_state.shape[3]
    lat_total = row_order.shape[0]
    mode_total = mode_order.shape[0]
    weights = row_weights(row_order, lat_total)
    summed = jnp.einsum("kla,sklc->sakc", legendre, spec_cot, preferred_element_type=jnp.float32)
    fourier_cot = (summed * weights[None, :, None, None]).astype(jnp.bfloat16)
    fourier_rows = lax.all_to_all(fourier_cot, "wide", split_axis=1, concat_axis=2, tiled=True)
    cot_parts = fourier_rows.reshape(samples, lat_local, mode_total, 2, channels)
    grid_cot = jnp.einsum(
        "sakpc,kpl->salc",
        cot_parts,
        back_table(mode_order, lon_total),
        preferred_element_type=jnp.float32,
    ).astype(jnp.bfloat16)
    state_rows = grid_state.reshape(-1, channels)
    cot_rows = grid_cot.reshape(-1, channels)
    preact = jnp.dot(state_rows, weight_in, preferred_element_type=jnp.float32) + bias_in
    sigmoid_pre = jax.nn.sigmoid(preact)
    activation = (preact * sigmoid_pre).astype(jnp.bfloat16)
    back_hidden = jnp.einsum("rc,hc->rh", cot_rows, weight_out, preferred_element_type=jnp.float32)
    grad_preact = (back_hidden * sigmoid_pre * (1.0 + preact * (1.0 - sigmoid_pre))).astype(
        jnp.bfloat16
    )
    dstate = jnp.einsum(
        "rh,ch->rc", grad_preact, weight_in, preferred_element_type=jnp.float32
    ).astype(jnp.bfloat16)
    local_in = jnp.einsum("rc,rh->ch", state_rows, grad_preact, preferred_element_type=jnp.float32)
    local_bias = jnp.sum(grad_preact.astype(jnp.float32), axis=0)
    local_out = jnp.einsum("rh,rc->hc", activation, cot_rows, preferred_element_type=jnp.float32)
    grad_weight_in, grad_bias_in, grad_weight_out = lax.psum(
        (local_in, local_bias, local_out), ("dp", "wide")
    )
    dstate_grid = dstate.reshape(samples, lat_local, lon_total, channels)
    fourier_grad = jnp.einsum(
        "salc,lkp->sakpc",
        dstate_grid,
        forward_table(mode_order, lon_total),
        preferred_element_type=jnp.float32,
    ).astype(jnp.bfloat16)
    fourier_grad = fourier_grad.reshape(samples, lat_local, mode_total, 2 * channels)
    gathered = lax.all_to_all(fourier_grad, "wide", split_axis=2, concat_axis=1, tiled=True)
    spec_grad = jnp.einsum(
        "kla,sakc->sklc", legendre, gathered, preferred_element_type=jnp.float32
    ).astype(jnp.bfloat16)
    return (spec_grad, grad_weight_in, grad_bias_in, grad_weight_out)


def solution(mesh):
    placed = (
        P("dp", "wide", None, None),
        P("dp", "wide", None, None),
        P(),
        P(),
        P(),
        P("wide", None, None),
        P(),
        P(),
    )
    return jax.shard_map(
        per_device,
        mesh=mesh,
        in_specs=placed,
        out_specs=(P("dp", "wide", None, None), P(), P(), P()),
        check_vma=False,
    )
```

profile of v0, /device:TPU:1, one launch (start us, length us, event | category | flops | bytes accessed | tf_op | source)
XLA Modules:
  0.0 344.5 jit_solution(13337079491292806313)
XLA Ops:
  7.2 0.0 copy-start
  7.2 0.8 fusion.34
  8.0 0.3 copy-done
  8.2 1.3 fusion.7
  9.5 1.9 copy.23
  11.4 16.5 %all-to-all-start = ((bf16[1,512,2,296]{3,2,0,1:T(2,128)(2,1)}), bf16[1,512,2,296]{3,2,0,1:T(2,128)(2,1)S(1)}, u32[]{:S(2)}, u32[]{:S(2)}) async-start(bf16[1,512,2,296]{3,2,0,1:T(2,128)(2,1)} %copy.23), calls=%async_computation | async-start | bytes 1572864 | tf_op jit(solution)/shard_map/all_to_all | solution.py:47
  27.9 0.0 copy-start.6
  27.9 1.8 pad.5
  29.7 0.0 copy-start.5
  29.7 0.0 copy-start.7
  29.7 0.5 copy.37
  30.2 0.0 copy-done.6
  30.2 5.5 %multiply_convert_fusion.5 = (bf16[256,1024,1]{0,1,2:T(8,128)(2,1)}, bf16[256,1024,1]{0,1,2:T(8,128)(2,1)}) fusion(s32[256]{0:T(256)S(1)} %copy-done.6, f32[256]{0:T(256)S(1)} %get-tuple-element.8, f32[256]{0:T(256)S(1)} %get-tuple-element.9), kind=kLoop, calls=%fused_computation.47 | loop fusion | flops 4718592 | bytes 1051648 | tf_op jit(solution)/shard_map/convert.2
  35.7 5.6 %multiply_convert_fusion.3 = (bf16[256,1,1024]{2,0,1:T(8,128)(2,1)}, bf16[256,1,1024]{2,0,1:T(8,128)(2,1)}) fusion(s32[256]{0:T(256)S(1)} %copy-done.6), kind=kLoop, calls=%fused_computation.43 | loop fusion | flops 4980736 | bytes 1049600 | tf_op jit(solution)/shard_map/convert
  41.3 0.0 copy-done.5
  41.3 0.0 copy-done.7
  41.3 2.7 convolution_add_fusion
  44.1 7.2 %all-to-all-done = bf16[1,512,2,296]{3,2,0,1:T(2,128)(2,1)S(1)} async-done(((bf16[1,512,2,296]{3,2,0,1:T(2,128)(2,1)}), bf16[1,512,2,296]{3,2,0,1:T(2,128)(2,1)S(1)}, u32[]{:S(2)}, u32[]{:S(2)}) %all-to-all-start) | async-done | bytes 606240 | tf_op jit(solution)/shard_map/all_to_all | solution.py:47
  51.3 0.5 copy.24
  51.9 1.8 reshape.295
  53.7 2.4 fusion.3
  56.1 0.9 copy.47
  57.0 0.0 copy-start.1
  57.0 0.0 copy-start.8
  57.0 0.5 pad.4
  57.5 0.5 copy.36
  58.0 0.0 copy-start.3
  58.0 1.6 copy-done.1
  59.7 1.9 convert_reduce_fusion
  61.6 0.0 copy-done.3
  61.6 1.3 copy-done.2
  62.9 0.8 convolution_convert_fusion
  63.8 1.8 reshape.298
  65.6 2.4 fusion.6
  68.0 1.2 copy.34
  69.3 1.7 reshape.305
  71.0 7.6 %all-to-all-start.1 = ((bf16[1,4,256,296]{3,1,0,2:T(4,128)(2,1)}), bf16[1,4,256,296]{3,1,0,2:T(4,128)(2,1)S(1)}, u32[]{:S(2)}, u32[]{:S(2)}) async-start(bf16[1,4,256,296]{3,1,0,2:T(4,128)(2,1)} %reshape.305), calls=%async_computation.1 | async-start | bytes 1572864 | tf_op jit(solution)/shard_map/all_to_all | solution.py:81
  78.6 0.0 all-reduce.3.cloned.1.call-start
  78.6 2.9 convolution_bitcast_fusion.1
  81.5 4.2 %fusion.2 = f32[256,148]{0,1:T(8,128)} fusion(bf16[4096,148]{0,1:T(8,128)(2,1)S(1)} %bitcast.90, f32[4096,256]{1,0:T(8,128)} %convolution_add_fusion), kind=kOutput, calls=%fused_computation.9 | convolution fusion | flops 315621376 | bytes 5558272 | tf_op jit(solution)/shard_map/rh,rc->hc/dot_general | solution.py:69
  85.8 0.0 all-reduce.3.cloned.1.call-update
  85.8 78.1 %psum.22 = f32[256]{0:T(256)} all-reduce(f32[256]{0:T(256)S(1)} %get-tuple-element.12), channel_id=1, replica_groups=mesh['dp'=2,'wide'=128] {'dp','wide'}, use_global_device_ids=true, to_apply=%region_2.3 | all-reduce | flops 256 | bytes 2048 | tf_op jit(solution)/shard_map/psum | solution.py:70
  163.9 0.0 all-to-all-done.1
  163.9 0.6 copy.30
  164.5 1.1 fusion.10
  165.6 168.9 %all-reduce.3.cloned.1.call-done = (f32[148,256]{1,0:T(8,128)}, f32[256,148]{0,1:T(8,128)}) async-done(((f32[148,256]{1,0:T(8,128)}, f32[256,148]{0,1:T(8,128)}), (f32[148,256]{1,0:T(8,128)}, f32[256,148]{0,1:T(8,128)})) %all-reduce.3.cloned.1.call-update) | async-done | bytes 303120 | tf_op jit(solution)/shard_map/psum | solution.py:70
  334.5 1.6 copy.50
  336.1 1.6 copy.51
  (5 shorter events, 0.0 us)
Async XLA Ops:
  7.2 1.1 copy-start
  11.4 39.9 %all-to-all-start = ((bf16[1,512,2,296]{3,2,0,1:T(2,128)(2,1)}), bf16[1,512,2,296]{3,2,0,1:T(2,128)(2,1)S(1)}, u32[]{:S(2)}, u32[]{:S(2)}) async-start(bf16[1,512,2,296]{3,2,0,1:T(2,128)(2,1)} %copy.23), calls=%async_computation | async-start | bytes 1572864 | tf_op jit(solution)/shard_map/all_to_all | solution.py:47
  27.9 2.3 copy-start.6
  29.7 11.7 %copy-start.5 = (bf16[148,256]{1,0:T(8,128)(2,1)S(1)}, bf16[148,256]{1,0:T(8,128)(2,1)}, u32[]{:S(2)}) copy-start(bf16[148,256]{1,0:T(8,128)(2,1)} %param.10) | copy-start | bytes 227332
  29.7 11.6 %copy-start.7 = (f32[256]{0:T(256)S(1)}, f32[256]{0:T(256)}, u32[]{:S(2)}) copy-start(f32[256]{0:T(256)} %param.11) | copy-start | bytes 3076
  57.0 2.6 copy-start.1
  57.0 2.6 copy-start.8
  58.0 3.6 %copy-start.3 = (bf16[19,8,4,1024]{3,1,2,0:T(8,128)(2,1)}, bf16[19,8,4,1024]{3,1,2,0:T(8,128)(2,1)S(1)}, u32[]{:S(2)}) copy-start(bf16[19,8,4,1024]{3,1,2,0:T(8,128)(2,1)S(1)} %copy.36) | copy-start | bytes 3735556
  61.6 1.3 copy-start.2
  71.0 92.8 %all-to-all-start.1 = ((bf16[1,4,256,296]{3,1,0,2:T(4,128)(2,1)}), bf16[1,4,256,296]{3,1,0,2:T(4,128)(2,1)S(1)}, u32[]{:S(2)}, u32[]{:S(2)}) async-start(bf16[1,4,256,296]{3,1,0,2:T(4,128)(2,1)} %reshape.305), calls=%async_computation.1 | async-start | bytes 1572864 | tf_op jit(solution)/shard_map/all_to_all | solution.py:81
  78.6 255.9 %all-reduce.3.cloned.1.call-start = ((), (), s32[]{:S(2)}) async-start(), calls=%async_computation.2 | async-start | bytes 622592 | tf_op jit(solution)/shard_map/psum | solution.py:70
  78.6 2.9 copy-start.4
Sparse Core Ops, SparseCore 0:
  85.9 248.5 all-reduce.2
where the time goes:
time: 345 us
  waiting for transfers between devices  176 us (51%)
  blocking collectives  78.1 us (23%)
  starting transfers between devices  24.1 us (7%)
  local copies, waits for them, and re-layouts  20.2 us (6%)
  matrix products  19.8 us (6%)
  between operations  14.2 us (4%)
  other arithmetic  11.9 us (3%)
    psum x1, waiting for transfers between devices, per_device(): lax.psum((local_in, local_bias, local_out), ('dp', 'wide'))  169 us
    psum x1, blocking collectives, per_device(): lax.psum((local_in, local_bias, local_out), ('dp', 'wide'))  78.1 us
    all_to_all x1, starting transfers between devices, per_device(): lax.all_to_all(fourier_cot, 'wide', split_axis=1, concat_axis=2, tiled=True)  16.5 us
    another operation x2, other arithmetic  11.1 us
    unnamed x24, local copies, waits for them, and re-layouts  9.65 us
    all_to_all x1, starting transfers between devices, per_device(): lax.all_to_all(fourier_grad, 'wide', split_axis=2, concat_axis=1, tiled=T...  7.58 us
    all_to_all x1, waiting for transfers between devices, per_device(): lax.all_to_all(fourier_cot, 'wide', split_axis=1, concat_axis=2, tiled=True)  7.23 us
  transfers between devices with their start and end apart: 3, of which 2 were waited for; matrix products, arithmetic and copies ran while one was open for 7% of the time, Pallas kernels for 0%

commit v1 on v0

--- a/solution.py
+++ b/solution.py
@@ -30,6 +30,24 @@
     multiple = jnp.where(mode_order == 0, 1.0, 2.0)[:, None]
     stacked = jnp.stack([multiple * jnp.cos(angles), -multiple * jnp.sin(angles)], axis=2)
     return jnp.transpose(stacked, (1, 0, 2)).astype(jnp.bfloat16)
+
+
+def sum_everywhere(*terms):
+    shards = lax.axis_size("wide")
+    flat = jnp.concatenate([term.reshape(-1) for term in terms])
+    size = flat.shape[0]
+    width = -(-size // (shards * 128)) * 128
+    blocks = jnp.pad(flat, (0, shards * width - size)).reshape(shards, width)
+    pieces = lax.all_to_all(blocks, "wide", split_axis=0, concat_axis=0, tiled=True)
+    part = jnp.sum(pieces, axis=0)
+    part = part + lax.ppermute(part, "dp", [(0, 1), (1, 0)])
+    spread = jnp.broadcast_to(part[None], (shards, width))
+    whole = lax.all_to_all(spread, "wide", split_axis=0, concat_axis=0, tiled=True).reshape(-1)
+    out, start = [], 0
+    for term in terms:
+        out.append(whole[start : start + term.size].reshape(term.shape))
+        start += term.size
+    return out
 
 
 def per_device(
@@ -67,9 +85,7 @@
     local_in = jnp.einsum("rc,rh->ch", state_rows, grad_preact, preferred_element_type=jnp.float32)
     local_bias = jnp.sum(grad_preact.astype(jnp.float32), axis=0)
     local_out = jnp.einsum("rh,rc->hc", activation, cot_rows, preferred_element_type=jnp.float32)
-    grad_weight_in, grad_bias_in, grad_weight_out = lax.psum(
-        (local_in, local_bias, local_out), ("dp", "wide")
-    )
+    grad_weight_in, grad_bias_in, grad_weight_out = sum_everywhere(local_in, local_bias, local_out)
     dstate_grid = dstate.reshape(samples, lat_local, lon_total, channels)
     fourier_grad = jnp.einsum(
         "salc,lkp->sakpc",

time: 345 us -> 145 us (0.42)
  waiting for transfers between devices: 176 us -> 43.7 us
  blocking collectives: 78.1 us -> 0 us
  starting transfers between devices: 24.1 us -> 48.3 us
  between operations: 14.2 us -> 0.89 us
  matrix products: 19.8 us -> 15.1 us
    psum x1 -> x0, waiting for transfers between devices: 169 us -> none  [per_device(): lax.psum((local_in, local_bias, local_out), ('dp', 'wide'))]
    psum x1 -> x0, blocking collectives: 78.1 us -> none  [per_device(): lax.psum((local_in, local_bias, local_out), ('dp', 'wide'))]
    all_to_all x1, waiting for transfers between devices: 0.01 us -> 17.9 us  [per_device(): lax.all_to_all(fourier_grad, 'wide', split_axis=2, concat_axis=1, tiled=T...]
    all_to_all x0 -> x2, starting transfers between devices: none -> 15.6 us  [the longest x1 8.04 us: sum_everywhere(): lax.all_to_all(spread, 'wide', split_axis=0, concat_axis=0, tiled=True)]
    all_to_all x0 -> x2, waiting for transfers between devices: none -> 11.5 us  [the longest x1 11.5 us: sum_everywhere(): lax.all_to_all(spread, 'wide', split_axis=0, concat_axis=0, tiled=True)]
    all_to_all x1, waiting for transfers between devices: 7.23 us -> 13.4 us  [per_device(): lax.all_to_all(fourier_cot, 'wide', split_axis=1, concat_axis=2, tiled=True)]
    all_to_all x1, starting transfers between devices: 7.58 us -> 13.2 us  [per_device(): lax.all_to_all(fourier_grad, 'wide', split_axis=2, concat_axis=1, tiled=T...]
    unnamed x24 -> x23, local copies, waits for them, and re-layouts: 9.65 us -> 5.53 us
  transfers between devices with their start and end apart: 3 -> 5, of which waited for: 2 -> 4; matrix products, arithmetic and copies ran while one was open for 7% -> 19% of each run, Pallas kernels for 0% -> 0%
where the time goes in v1:
time: 145 us; the launch traced here: 143 us
  starting transfers between devices  48.3 us (33%)
  waiting for transfers between devices  43.7 us (30%)
  local copies, waits for them, and re-layouts  19.9 us (14%)
  matrix products  15.1 us (10%)
  other arithmetic  14.8 us (10%)
    all_to_all x1, waiting for transfers between devices, per_device(): lax.all_to_all(fourier_grad, 'wide', split_axis=2, concat_axis=1, tiled=T...  17.9 us
    all_to_all x1, starting transfers between devices, per_device(): lax.all_to_all(fourier_cot, 'wide', split_axis=1, concat_axis=2, tiled=True)  16.5 us
    all_to_all x1, waiting for transfers between devices, per_device(): lax.all_to_all(fourier_cot, 'wide', split_axis=1, concat_axis=2, tiled=True)  13.4 us
    all_to_all x1, starting transfers between devices, per_device(): lax.all_to_all(fourier_grad, 'wide', split_axis=2, concat_axis=1, tiled=T...  13.2 us
    another operation x2, other arithmetic  11.7 us
    all_to_all x1, waiting for transfers between devices, sum_everywhere(): lax.all_to_all(spread, 'wide', split_axis=0, concat_axis=0, tiled=True)  11.5 us
    all_to_all x1, starting transfers between devices, sum_everywhere(): lax.all_to_all(spread, 'wide', split_axis=0, concat_axis=0, tiled=True)  8.04 us
    all_to_all x1, starting transfers between devices, sum_everywhere(): lax.all_to_all(blocks, 'wide', split_axis=0, concat_axis=0, tiled=True)  7.57 us
  transfers between devices with their start and end apart: 5, of which 4 were waited for; matrix products, arithmetic and copies ran while one was open for 19% of the time, Pallas kernels for 0%

profile of v1, /device:TPU:1, one launch (start us, length us, event | category | flops | bytes accessed | tf_op | source)
XLA Modules:
  0.0 142.6 jit_solution(1676678982138316871)
XLA Ops:
  0.6 0.0 copy-start
  0.6 0.8 fusion.34
  1.4 0.3 copy-done
  1.7 1.4 fusion.7
  3.1 1.9 %copy.47 = bf16[1,512,2,296]{3,2,0,1:T(2,128)(2,1)} copy(bf16[1,512,2,296]{1,3,2,0:T(8,128)(2,1)S(1)} %fusion.7) | data formatting | bytes 1212416 | tf_op jit(solution)/shard_map/convert_element_type | solution.py:64
  4.9 16.5 %all-to-all-start = ((bf16[1,512,2,296]{3,2,0,1:T(2,128)(2,1)}), bf16[1,512,2,296]{3,2,0,1:T(2,128)(2,1)S(1)}, u32[]{:S(2)}, u32[]{:S(2)}) async-start(bf16[1,512,2,296]{3,2,0,1:T(2,128)(2,1)} %copy.47), calls=%async_computation | async-start | bytes 1572864 | tf_op jit(solution)/shard_map/all_to_all | solution.py:65
  21.5 0.5 pad.16
  22.0 0.5 copy.66
  22.5 0.6 compare_select_fusion
  23.1 5.6 %multiply_convert_fusion.3 = (bf16[256,1,1024]{2,0,1:T(8,128)(2,1)}, bf16[256,1,1024]{2,0,1:T(8,128)(2,1)}) fusion(s32[256]{0:T(256)S(1)} %copy-done.6), kind=kLoop, calls=%fused_computation.43 | loop fusion | flops 4980736 | bytes 1049600 | tf_op jit(solution)/shard_map/convert
  28.7 2.7 %convolution_add_fusion = f32[4096,256]{1,0:T(8,128)} fusion(bf16[4096,148]{0,1:T(8,128)(2,1)S(1)} %bitcast.83, bf16[148,256]{1,0:T(8,128)(2,1)S(1)} %copy-done.5, f32[256]{0:T(256)S(1)} %copy-done.7), kind=kOutput, calls=%fused_computation | convolution fusion | flops 311427072 | bytes 5483520 | tf_op jit(solution)/shard_map/dot_general | solution.py:75
  31.5 13.4 %all-to-all-done = bf16[1,512,2,296]{3,2,0,1:T(2,128)(2,1)S(1)} async-done(((bf16[1,512,2,296]{3,2,0,1:T(2,128)(2,1)}), bf16[1,512,2,296]{3,2,0,1:T(2,128)(2,1)S(1)}, u32[]{:S(2)}, u32[]{:S(2)}) %all-to-all-start) | async-done | bytes 606240 | tf_op jit(solution)/shard_map/all_to_all | solution.py:65
  44.9 0.5 copy.48
  45.4 1.8 %reshape.321 = bf16[4,256,2,148]{3,2,1,0:T(2,128)(2,1)} reshape(bf16[1,4,128,2,296]{4,3,2,1,0:T(2,128)(2,1)S(1)} %copy.48) | data formatting | bytes 1212416 | tf_op jit(solution)/shard_map/reshape.4
  47.2 2.4 %fusion.3 = bf16[1,4,1024,148]{2,3,1,0:T(8,128)(2,1)S(1)} fusion(bf16[256,1,1024]{2,0,1:T(8,128)(2,1)} %get-tuple-element.25, bf16[256,1,1024]{2,0,1:T(8,128)(2,1)} %get-tuple-element.24, bf16[4,256,2,148]{3,2,1,0:T(2,128)(2,1)} %reshape.321), kind=kOutput, calls=%fused_computation.16 | convolution fusion | flops 623460352 | bytes 2867200 | tf_op jit(solution)/shard_map/sakpc,kpl->salc/dot_general | solution.py:67
  49.6 0.9 copy.76
  50.6 0.5 pad.15
  51.1 0.5 copy.65
  51.6 1.2 copy-done.1
  52.8 1.3 fusion.2
  54.1 1.9 %convert_reduce_fusion = (f32[256]{0:T(256)S(1)}, bf16[4096,256]{1,0:T(8,128)(2,1)S(1)}) fusion(f32[4096,256]{1,0:T(8,128)S(1)} %copy-done.1, bf16[4096,148]{0,1:T(8,128)(2,1)S(1)} %bitcast.94, bf16[256,148]{0,1:T(8,128)(2,1)S(1)} %copy-done.8), kind=kOutput, calls=%fused_computation.6 | convolution fusion | flops 321912576 | bytes 7580672 | tf_op jit(solution)/shard_map/rc,hc->rh/dot_general | solution.py:78
  56.0 1.3 copy-done.2
  57.3 0.5 convolution_bitcast_fusion.1
  57.9 0.2 reshape.328
  58.1 0.8 select_maximum_fusion
  58.9 7.6 %all-to-all-start.2 = ((f32[128,1,640]{2,1,0:T(1,128)}), f32[128,1,640]{2,1,0:T(1,128)S(1)}, u32[]{:S(2)}, u32[]{:S(2)}) async-start(f32[128,1,640]{2,1,0:T(1,128)} %bitcast.22), calls=%async_computation.2 | async-start | bytes 655360 | tf_op jit(solution)/shard_map/all_to_all | solution.py:41
  66.4 6.0 %multiply_convert_fusion.5 = (bf16[256,1024,1]{0,1,2:T(8,128)(2,1)S(1)}, bf16[256,1024,1]{0,1,2:T(8,128)(2,1)}) fusion(s32[256]{0:T(256)S(1)} %copy-done.6, f32[256]{0:T(256)} %get-tuple-element.22, f32[256]{0:T(256)} %get-tuple-element.23), kind=kLoop, calls=%fused_computation.47 | loop fusion | flops 4718592 | bytes 1051648 | tf_op jit(solution)/shard_map/convert.2
  72.5 1.9 %convolution_convert_fusion = bf16[4096,148]{0,1:T(8,128)(2,1)} fusion(bf16[4096,256]{1,0:T(8,128)(2,1)S(1)} %copy-done.3, bf16[148,256]{1,0:T(8,128)(2,1)S(1)} %copy-done.5), kind=kOutput, calls=%fused_computation.4 | convolution fusion | flops 310984704 | bytes 3385344 | tf_op jit(solution)/shard_map/rh,ch->rc/dot_general | solution.py:82
  74.4 3.1 %reshape.324 = bf16[4,1024,148]{1,0,2:T(4,128)(2,1)S(1)} reshape(bf16[4096,148]{0,1:T(8,128)(2,1)} %convolution_convert_fusion) | data formatting | bytes 2424832 | tf_op jit(solution)/shard_map/reshape.6
  77.4 1.9 %fusion.6 = bf16[1,4,256,2,148]{2,4,1,3,0:T(8,128)(2,1)S(1)} fusion(bf16[4,1024,148]{1,0,2:T(4,128)(2,1)S(1)} %reshape.324, bf16[256,1024,1]{0,1,2:T(8,128)(2,1)} %get-tuple-element.21, bf16[256,1024,1]{0,1,2:T(8,128)(2,1)S(1)} %get-tuple-element.20), kind=kOutput, calls=%fused_computation.21 | convolution fusion | flops 623157248 | bytes 2867200 | tf_op jit(solution)/shard_map/salc,lkp->sakpc/dot_general | solution.py:90
  79.3 1.0 copy.62
  80.3 1.7 %reshape.335 = bf16[1,4,256,296]{3,1,0,2:T(4,128)(2,1)} reshape(bf16[1,4,256,2,148]{4,3,1,2,0:T(2,128)(2,1)S(1)} %copy.62) | data formatting | bytes 1212416 | tf_op jit(solution)/shard_map/reshape | solution.py:96
  82.0 13.2 %all-to-all-start.1 = ((bf16[1,4,256,296]{3,1,0,2:T(4,128)(2,1)}), bf16[1,4,256,296]{3,1,0,2:T(4,128)(2,1)S(1)}, u32[]{:S(2)}, u32[]{:S(2)}) async-start(bf16[1,4,256,296]{3,1,0,2:T(4,128)(2,1)} %reshape.335), calls=%async_computation.1 | async-start | bytes 1572864 | tf_op jit(solution)/shard_map/all_to_all | solution.py:97
  95.2 0.2 reduce_sum.19
  95.5 2.9 %collective-permute-start = (f32[640]{0:T(1024)S(1)}, f32[640]{0:T(1024)S(1)}, u32[]{:S(2)}, u32[]{:S(2)}) collective-permute-start(f32[640]{0:T(1024)S(1)} %reduce_sum.19), channel_id=1, source_target_pairs={{0,128},{128,0},{1,129},{129,1},{2,130},{130,2},{3,131},{131,3},{4... | collective-permute-start | bytes 7688 | tf_op jit(solution)/shard_map/ppermute | solution.py:43
  98.4 0.8 collective-permute-done
  99.3 17.9 %all-to-all-done.1 = bf16[1,4,256,296]{3,1,0,2:T(4,128)(2,1)S(1)} async-done(((bf16[1,4,256,296]{3,1,0,2:T(4,128)(2,1)}), bf16[1,4,256,296]{3,1,0,2:T(4,128)(2,1)S(1)}, u32[]{:S(2)}, u32[]{:S(2)}) %all-to-all-start.1) | async-done | bytes 606240 | tf_op jit(solution)/shard_map/all_to_all | solution.py:97
  117.1 0.9 broadcast_in_dim.10
  118.0 8.0 %all-to-all-start.3 = ((f32[128,1,640]{2,1,0:T(1,128)}), f32[128,1,640]{2,1,0:T(1,128)S(1)}, u32[]{:S(2)}, u32[]{:S(2)}) async-start(f32[128,1,640]{2,1,0:T(1,128)} %broadcast_in_dim.10), calls=%async_computation.3 | async-start | bytes 655360 | tf_op jit(solution)/shard_map/all_to_all | solution.py:45
  126.1 0.6 copy.54
  126.7 1.1 fusion.10
  127.8 11.5 %all-to-all-done.3 = f32[128,1,640]{2,1,0:T(1,128)S(1)} async-done(((f32[128,1,640]{2,1,0:T(1,128)}), f32[128,1,640]{2,1,0:T(1,128)S(1)}, u32[]{:S(2)}, u32[]{:S(2)}) %all-to-all-start.3) | async-done | bytes 327712 | tf_op jit(solution)/shard_map/all_to_all | solution.py:45
  139.4 0.6 slice.17
  139.9 0.3 reshape.330
  140.3 0.8 copy.58
  141.0 0.8 reduce.1
  141.8 0.1 slice.12
  141.9 0.7 slice.16
  (18 shorter events, 0.1 us)
Async XLA Ops:
  0.6 1.1 copy-start
  1.7 19.8 %copy-start.4 = (bf16[1,4,1024,148]{2,1,3,0:T(4,128)(2,1)S(1)}, bf16[1,4,1024,148]{2,1,3,0:T(4,128)(2,1)}, u32[]{:S(2)}) copy-start(bf16[1,4,1024,148]{2,1,3,0:T(4,128)(2,1)} %param.9) | copy-start | bytes 3637252
  4.9 39.9 %all-to-all-start = ((bf16[1,512,2,296]{3,2,0,1:T(2,128)(2,1)}), bf16[1,512,2,296]{3,2,0,1:T(2,128)(2,1)S(1)}, u32[]{:S(2)}, u32[]{:S(2)}) async-start(bf16[1,512,2,296]{3,2,0,1:T(2,128)(2,1)} %copy.47), calls=%async_computation | async-start | bytes 1572864 | tf_op jit(solution)/shard_map/all_to_all | solution.py:65
  21.5 1.0 copy-start.6
  22.0 6.7 %copy-start.5 = (bf16[148,256]{1,0:T(8,128)(2,1)S(1)}, bf16[148,256]{1,0:T(8,128)(2,1)}, u32[]{:S(2)}) copy-start(bf16[148,256]{1,0:T(8,128)(2,1)} %param.10) | copy-start | bytes 227332
  22.0 6.7 %copy-start.7 = (f32[256]{0:T(256)S(1)}, f32[256]{0:T(256)}, u32[]{:S(2)}) copy-start(f32[256]{0:T(256)} %param.11) | copy-start | bytes 3076
  50.6 2.2 %copy-start.1 = (f32[4096,256]{1,0:T(8,128)S(1)}, f32[4096,256]{1,0:T(8,128)}, u32[]{:S(2)}) copy-start(f32[4096,256]{1,0:T(8,128)} %convolution_add_fusion) | copy-start | bytes 12582916
  52.8 1.3 copy-start.8
  56.0 1.3 copy-start.2
  57.8 14.6 %copy-start.3 = (bf16[4096,256]{1,0:T(8,128)(2,1)S(1)}, bf16[4096,256]{1,0:T(8,128)(2,1)}, u32[]{:S(2)}) copy-start(bf16[4096,256]{1,0:T(8,128)(2,1)} %copy-done.2) | copy-start | bytes 6291460
  58.9 23.2 %all-to-all-start.2 = ((f32[128,1,640]{2,1,0:T(1,128)}), f32[128,1,640]{2,1,0:T(1,128)S(1)}, u32[]{:S(2)}, u32[]{:S(2)}) async-start(f32[128,1,640]{2,1,0:T(1,128)} %bitcast.22), calls=%async_computation.2 | async-start | bytes 655360 | tf_op jit(solution)/shard_map/all_to_all | solution.py:41
  82.0 35.1 %all-to-all-start.1 = ((bf16[1,4,256,296]{3,1,0,2:T(4,128)(2,1)}), bf16[1,4,256,296]{3,1,0,2:T(4,128)(2,1)S(1)}, u32[]{:S(2)}, u32[]{:S(2)}) async-start(bf16[1,4,256,296]{3,1,0,2:T(4,128)(2,1)} %reshape.335), calls=%async_computation.1 | async-start | bytes 1572864 | tf_op jit(solution)/shard_map/all_to_all | solution.py:97
  95.5 3.8 %collective-permute-start = (f32[640]{0:T(1024)S(1)}, f32[640]{0:T(1024)S(1)}, u32[]{:S(2)}, u32[]{:S(2)}) collective-permute-start(f32[640]{0:T(1024)S(1)} %reduce_sum.19), channel_id=1, source_target_pairs={{0,128},{128,0},{1,129},{129,1},{2,130},{130,2},{3,131},{131,3},{4... | collective-permute-start | bytes 7688 | tf_op jit(solution)/shard_map/ppermute | solution.py:43
  118.0 21.4 %all-to-all-start.3 = ((f32[128,1,640]{2,1,0:T(1,128)}), f32[128,1,640]{2,1,0:T(1,128)S(1)}, u32[]{:S(2)}, u32[]{:S(2)}) async-start(f32[128,1,640]{2,1,0:T(1,128)} %broadcast_in_dim.10), calls=%async_computation.3 | async-start | bytes 655360 | tf_op jit(solution)/shard_map/all_to_all | solution.py:45

commit v2 on v1

--- a/solution.py
+++ b/solution.py
@@ -1,9 +1,92 @@
+import functools
 import math
 
 import jax
 import jax.numpy as jnp
 from jax import lax
+from jax.experimental import pallas as pl
+from jax.experimental.pallas import tpu as pltpu
 from jax.sharding import PartitionSpec as P
+
+
+MESH = pl.DeviceIdType.MESH
+PLANE = 16
+
+
+def exchange_kernel(n, x_ref, o_ref, send_sem, recv_sem, own_sem, ready):
+    me = lax.axis_index("wide")
+    lines = n // PLANE
+    line, spot = me // PLANE, me % PLANE
+
+    def along(t):
+        return {"wide": (line + t) % lines * PLANE + spot}
+
+    def across(t):
+        return {"wide": line * PLANE + (spot + t) % PLANE}
+
+    barrier = pltpu.get_barrier_semaphore()
+
+    @pl.loop(1, lines)
+    def _(t):
+        pl.semaphore_signal(barrier, inc=1, device_id=along(t), device_id_type=MESH)
+
+    @pl.loop(1, PLANE)
+    def _(t):
+        pl.semaphore_signal(barrier, inc=1, device_id=across(t), device_id_type=MESH)
+
+    own = pltpu.make_async_copy(x_ref.at[me], o_ref.at[me], own_sem)
+    own.start()
+    pl.semaphore_wait(barrier, lines + PLANE - 2)
+
+    @pl.loop(1, PLANE)
+    def _(t):
+        pl.semaphore_signal(ready, inc=1, device_id=across(t), device_id_type=MESH)
+
+    pl.semaphore_wait(ready, PLANE - 1)
+
+    @pl.loop(1, n)
+    def _(t):
+        to = (line + t) % lines * PLANE + (spot + t // lines) % PLANE
+        pltpu.make_async_remote_copy(
+            x_ref.at[to],
+            o_ref.at[me],
+            send_sem,
+            recv_sem,
+            device_id={"wide": to},
+            device_id_type=MESH,
+        ).start()
+
+    own.wait()
+    rest = pltpu.make_async_remote_copy(
+        x_ref.at[pl.ds(0, n - 1)],
+        o_ref.at[pl.ds(0, n - 1)],
+        send_sem,
+        recv_sem,
+        device_id=across(1),
+        device_id_type=MESH,
+    )
+    rest.wait_send()
+    rest.wait_recv()
+
+
+def exchange(x, number):
+    n = x.shape[0]
+    return pl.pallas_call(
+        functools.partial(exchange_kernel, n),
+        name=f"exchange_{number}",
+        out_shape=jax.ShapeDtypeStruct(x.shape, x.dtype),
+        in_specs=[pl.BlockSpec(memory_space=pltpu.VMEM)],
+        out_specs=pl.BlockSpec(memory_space=pltpu.VMEM),
+        scratch_shapes=[
+            pltpu.SemaphoreType.DMA(()),
+            pltpu.SemaphoreType.DMA(()),
+            pltpu.SemaphoreType.DMA(()),
+            pltpu.SemaphoreType.REGULAR,
+        ],
+        compiler_params=pltpu.CompilerParams(
+            collective_id=number, has_side_effects=True, vmem_limit_bytes=32 * 2**20
+        ),
+    )(x)
 
 
 def row_weights(row_order, lat_total):
@@ -38,11 +121,11 @@
     size = flat.shape[0]
     width = -(-size // (shards * 128)) * 128
     blocks = jnp.pad(flat, (0, shards * width - size)).reshape(shards, width)
-    pieces = lax.all_to_all(blocks, "wide", split_axis=0, concat_axis=0, tiled=True)
+    pieces = exchange(blocks.reshape(shards, width // 128, 128), 3)
     part = jnp.sum(pieces, axis=0)
     part = part + lax.ppermute(part, "dp", [(0, 1), (1, 0)])
-    spread = jnp.broadcast_to(part[None], (shards, width))
-    whole = lax.all_to_all(spread, "wide", split_axis=0, concat_axis=0, tiled=True).reshape(-1)
+    spread = jnp.broadcast_to(part[None], (shards, width // 128, 128))
+    whole = exchange(spread, 4).reshape(-1)
     out, start = [], 0
     for term in terms:
         out.append(whole[start : start + term.size].reshape(term.shape))
@@ -62,8 +145,14 @@
     weights = row_weights(row_order, lat_total)
     summed = jnp.einsum("kla,sklc->sakc", legendre, spec_cot, preferred_element_type=jnp.float32)
     fourier_cot = (summed * weights[None, :, None, None]).astype(jnp.bfloat16)
-    fourier_rows = lax.all_to_all(fourier_cot, "wide", split_axis=1, concat_axis=2, tiled=True)
-    cot_parts = fourier_rows.reshape(samples, lat_local, mode_total, 2, channels)
+    shards = lat_total // lat_local
+    own_modes = mode_total // shards
+    packed = fourier_cot.reshape(shards, lat_local, own_modes * 2 * channels)
+    packed = jnp.pad(packed, ((0, 0), (0, 0), (0, -packed.shape[2] % 128)))
+    fourier_rows = exchange(packed, 1)[:, :, : own_modes * 2 * channels]
+    cot_parts = jnp.swapaxes(fourier_rows, 0, 1).reshape(
+        samples, lat_local, mode_total, 2, channels
+    )
     grid_cot = jnp.einsum(
         "sakpc,kpl->salc",
         cot_parts,
@@ -93,8 +182,10 @@
         forward_table(mode_order, lon_total),
         preferred_element_type=jnp.float32,
     ).astype(jnp.bfloat16)
-    fourier_grad = fourier_grad.reshape(samples, lat_local, mode_total, 2 * channels)
-    gathered = lax.all_to_all(fourier_grad, "wide", split_axis=2, concat_axis=1, tiled=True)
+    packed = fourier_grad.reshape(lat_local, shards, own_modes * 2 * channels)
+    packed = jnp.pad(jnp.swapaxes(packed, 0, 1), ((0, 0), (0, 0), (0, -packed.shape[2] % 128)))
+    gathered = exchange(packed, 2)[:, :, : own_modes * 2 * channels]
+    gathered = gathered.reshape(samples, lat_total, own_modes, 2 * channels)
     spec_grad = jnp.einsum(
         "kla,sakc->sklc", legendre, gathered, preferred_element_type=jnp.float32
     ).astype(jnp.bfloat16)

time: 145 us -> 129 us (0.89); the launches traced: 143 us -> 128 us
  Pallas kernels: 0 us -> 87.1 us
  starting transfers between devices: 48.3 us -> 3.7 us
  waiting for transfers between devices: 43.7 us -> 0.01 us
  local copies, waits for them, and re-layouts: 19.9 us -> 14.5 us
  matrix products: 15.1 us -> 11 us
  other arithmetic: 14.8 us -> 11 us
    pallas_call x0 -> x4, Pallas kernels: none -> 87.1 us  [exchange(): pl.pallas_call(functools.partial(exchange_kernel, n), name=f'exchange_{nu...]
    all_to_all x4 -> x0, starting transfers between devices: 45.3 us -> none  [the longest x1 16.5 us: per_device(): lax.all_to_all(fourier_cot, 'wide', split_axis=1, concat_axis=2, tiled=True)]
    all_to_all x4 -> x0, waiting for transfers between devices: 42.8 us -> none  [the longest x1 17.9 us: per_device(): lax.all_to_all(fourier_grad, 'wide', split_axis=2, concat_axis=1, tiled=T...]
    another operation x2 -> x4, local copies, waits for them, and re-layouts: 4.86 us -> 2.39 us
    dot_general x1, matrix products: 2.74 us -> 0.8 us  [per_device(): jnp.dot(state_rows, weight_in, preferred_element_type=jnp.float32) + bias_in]
    another operation x2, other arithmetic: 11.7 us -> 10.1 us
    dot_general x1, matrix products: 2.4 us -> 0.86 us  [per_device(): jnp.einsum('sakpc,kpl->salc', cot_parts, back_table(mode_order, lon_total...]
    unnamed x23 -> x19, local copies, waits for them, and re-layouts: 5.53 us -> 4.38 us
  transfers between devices with their start and end apart: 5 -> 1, of which waited for: 4 -> 0; matrix products, arithmetic and copies ran while one was open for 19% -> 10% of each run, Pallas kernels for 0% -> 19%
where the time goes in v2:
time: 129 us; the launch traced here: 128 us
  Pallas kernels  87.1 us (68%)
  local copies, waits for them, and re-layouts  14.5 us (11%)
  other arithmetic  11 us (9%)
  matrix products  11 us (9%)
  starting transfers between devices  3.7 us (3%)
    pallas_call x4, Pallas kernels, exchange(): pl.pallas_call(functools.partial(exchange_kernel, n), name=f'exchange_{nu...  87.1 us
    another operation x2, other arithmetic  10.1 us
    unnamed x19, local copies, waits for them, and re-layouts  4.38 us
    ppermute x1, starting transfers between devices, sum_everywhere(): part = part + lax.ppermute(part, 'dp', [(0, 1), (1, 0)])  3.7 us
  transfers between devices with their start and end apart: 1, of which 0 were waited for; matrix products, arithmetic and copies ran while one was open for 10% of the time, Pallas kernels for 19%

profile of v2, /device:TPU:1, one launch (start us, length us, event | category | flops | bytes accessed | tf_op | source)
XLA Modules:
  0.0 128.3 jit_solution(15931109600740310464)
XLA Ops:
  0.6 0.0 copy-start
  0.6 5.7 %multiply_convert_fusion.3 = (bf16[256,1,1024]{2,0,1:T(8,128)(2,1)S(1)}, bf16[256,1,1024]{2,0,1:T(8,128)(2,1)S(1)}) fusion(s32[256]{0:T(256)} %param.15), kind=kLoop, calls=%fused_computation.43 | loop fusion | flops 4980736 | bytes 1049600 | tf_op jit(solution)/shard_map/convert
  6.4 0.7 fusion.34
  7.1 1.3 %fusion.7 = bf16[1,512,2,296]{1,3,2,0:T(8,128)(2,1)S(1)} fusion(bf16[2,256,512]{2,1,0:T(8,128)(2,1)S(1)} %copy-done, f32[512]{0:T(512)S(1)} %fusion.34, bf16[1,2,256,296]{2,3,1,0:T(8,128)(2,1)} %param.8), kind=kOutput, calls=%fused_computation.22 | convolution fusion | flops 155795456 | bytes 1435648 | tf_op jit(solution)/shard_map/kla,sklc->sakc/dot_general | solution.py:146
  8.4 1.2 copy.15
  9.6 0.7 reshape.314
  10.3 0.3 pad.11.x_ref
  10.6 28.4 %exchange_1.1 = bf16[128,4,640]{2,1,0:T(4,128)(2,1)S(1)} custom-call(bf16[128,4,640]{2,1,0:T(4,128)(2,1)S(1)} %pad.11.x_ref), custom_call_target="tpu_custom_call" | custom-call | tf_op jit(solution)/shard_map/exchange_1/pallas_call | solution.py:74
  39.0 0.2 slice_bitcast_fusion
  39.2 0.1 copy.16
  39.3 0.7 reshape.315
  40.0 0.9 fusion.3
  40.9 0.9 copy.40
  41.8 0.0 copy-start.2
  41.8 0.5 pad.24
  42.3 0.5 copy.28
  42.8 0.3 copy-done.2
  43.1 0.5 pad.25
  43.6 0.5 copy.29
  44.1 0.8 convolution_add_fusion
  44.9 0.0 copy-start.6
  44.9 1.3 fusion.2
  46.2 1.9 %convert_reduce_fusion = (f32[256]{0:T(256)S(1)}, bf16[4096,256]{1,0:T(8,128)(2,1)S(1)}) fusion(f32[4096,256]{1,0:T(8,128)S(1)} %convolution_add_fusion, bf16[4096,148]{0,1:T(8,128)(2,1)S(1)} %bitcast.86, bf16[256,148]{0,1:T(8,128)(2,1)S(1)} %copy-done.6), kind=kOutput, calls=%fused_computation.6 | convolution fusion | flops 321912576 | bytes 7580672 | tf_op jit(solution)/shard_map/rc,hc->rh/dot_general | solution.py:167
  48.1 1.4 %copy-done.1 = bf16[4096,256]{1,0:T(8,128)(2,1)} copy-done((bf16[4096,256]{1,0:T(8,128)(2,1)}, bf16[4096,256]{1,0:T(8,128)(2,1)S(1)}, u32[]{:S(2)}) %copy-start.1) | copy-done | bytes 2097176
  49.5 0.5 convolution_bitcast_fusion.1
  50.0 0.2 reshape.322
  50.2 0.1 reshape_reshape.3.x_ref
  50.3 16.3 %exchange_3.1 = f32[128,5,128]{2,1,0:T(8,128)S(1)} custom-call(f32[128,5,128]{2,1,0:T(8,128)S(1)} %reshape_reshape.3.x_ref), custom_call_target="tpu_custom_call" | custom-call | tf_op jit(solution)/shard_map/exchange_3/pallas_call | solution.py:74
  66.6 0.0 copy-start.4
  66.6 0.1 reduce_sum.19
  66.7 3.7 %collective-permute-start = (f32[5,128]{1,0:T(8,128)S(1)}, f32[5,128]{1,0:T(8,128)S(1)}, u32[]{:S(2)}, u32[]{:S(2)}) collective-permute-start(f32[5,128]{1,0:T(8,128)S(1)} %reduce_sum.19), channel_id=1, source_target_pairs={{0,128},{128,0},{1,129},{129,1},{2,130},{130,2},{3,131},{131,3},{4... | collective-permute-start | bytes 7688 | tf_op jit(solution)/shard_map/ppermute | solution.py:126
  70.4 2.4 %convolution_convert_fusion = bf16[4096,148]{0,1:T(8,128)(2,1)S(1)} fusion(bf16[4096,256]{1,0:T(8,128)(2,1)} %copy-done.1, bf16[148,256]{1,0:T(8,128)(2,1)S(1)} %copy-done.3), kind=kOutput, calls=%fused_computation.4 | convolution fusion | flops 310984704 | bytes 3385344 | tf_op jit(solution)/shard_map/rh,ch->rc/dot_general | solution.py:171
  72.9 0.7 reshape.318
  73.6 4.4 %multiply_convert_fusion.5 = (bf16[256,1024,1]{0,1,2:T(8,128)(2,1)S(1)}, bf16[256,1024,1]{0,1,2:T(8,128)(2,1)S(1)}) fusion(s32[256]{0:T(256)S(1)} %copy-done.4, f32[256]{0:T(256)S(1)} %get-tuple-element.10, f32[256]{0:T(256)S(1)} %get-tuple-element.11), kind=kLoop, calls=%fused_computation.47 | loop fusion | flops 4718592 | bytes 1051648 | tf_op jit(solution)/shard_map/convert.2
  78.0 0.8 fusion.6
  78.8 0.9 copy.20
  79.7 0.7 reshape.319
  80.3 0.5 copy.41
  80.9 0.3 pad.12.x_ref
  81.1 24.2 %exchange_2.1 = bf16[128,4,640]{2,1,0:T(4,128)(2,1)S(1)} custom-call(bf16[128,4,640]{2,1,0:T(4,128)(2,1)S(1)} %pad.12.x_ref), custom_call_target="tpu_custom_call" | custom-call | tf_op jit(solution)/shard_map/exchange_2/pallas_call | solution.py:74
  105.3 0.9 reshape.320
  106.3 1.1 fusion.10
  107.4 18.3 %exchange_4.1 = f32[128,5,128]{2,1,0:T(8,128)S(1)} custom-call(f32[128,5,128]{2,1,0:T(8,128)S(1)} %broadcast_in_dim.10.x_ref), custom_call_target="tpu_custom_call" | custom-call | tf_op jit(solution)/shard_map/exchange_4/pallas_call | solution.py:74
  125.9 0.6 slice.25
  126.4 0.1 slice.20
  126.6 0.3 reshape.324
  126.9 0.8 copy.24
  127.7 0.7 slice.24
  (16 shorter events, 0.2 us)
Async XLA Ops:
  0.6 6.5 %copy-start = (bf16[2,256,512]{2,1,0:T(8,128)(2,1)S(1)}, bf16[2,256,512]{2,1,0:T(8,128)(2,1)}, u32[]{:S(2)}) copy-start(bf16[2,256,512]{2,1,0:T(8,128)(2,1)} %param.13) | copy-start | bytes 1572868
  41.8 1.3 %copy-start.2 = (bf16[1,4,1024,148]{2,1,3,0:T(4,128)(2,1)S(1)}, bf16[1,4,1024,148]{2,1,3,0:T(4,128)(2,1)}, u32[]{:S(2)}) copy-start(bf16[1,4,1024,148]{2,1,3,0:T(4,128)(2,1)} %param.9) | copy-start | bytes 3637252
  43.1 1.0 copy-start.3
  43.1 1.0 copy-start.5
  44.9 1.3 %copy-start.6 = (bf16[256,148]{0,1:T(8,128)(2,1)S(1)}, bf16[256,148]{0,1:T(8,128)(2,1)}, u32[]{:S(2)}) copy-start(bf16[256,148]{0,1:T(8,128)(2,1)} %param.12) | copy-start | bytes 227332
  48.1 1.4 %copy-start.1 = (bf16[4096,256]{1,0:T(8,128)(2,1)}, bf16[4096,256]{1,0:T(8,128)(2,1)S(1)}, u32[]{:S(2)}) copy-start(bf16[4096,256]{1,0:T(8,128)(2,1)S(1)} %get-tuple-element.15) | copy-start | bytes 6291460
  66.6 6.3 %copy-start.4 = (s32[256]{0:T(256)S(1)}, s32[256]{0:T(256)}, u32[]{:S(2)}) copy-start(s32[256]{0:T(256)} %param.15) | copy-start | bytes 3076
  66.7 40.7 %collective-permute-start = (f32[5,128]{1,0:T(8,128)S(1)}, f32[5,128]{1,0:T(8,128)S(1)}, u32[]{:S(2)}, u32[]{:S(2)}) collective-permute-start(f32[5,128]{1,0:T(8,128)S(1)} %reduce_sum.19), channel_id=1, source_target_pairs={{0,128},{128,0},{1,129},{129,1},{2,130},{130,2},{3,131},{131,3},{4... | collective-permute-start | bytes 7688 | tf_op jit(solution)/shard_map/ppermute | solution.py:126

commit v3 on v0

v3 whole, which is shorter than its diff:
```python
import functools
import math

import jax
import jax.numpy as jnp
from jax import lax
from jax.experimental import pallas as pl
from jax.experimental.pallas import tpu as pltpu
from jax.sharding import PartitionSpec as P

MESH = pl.DeviceIdType.MESH
F32 = jnp.float32
BF16 = jnp.bfloat16
CHUNKS = 2
LANES = 128
PLANE = 16
TURN = 2.0 * math.pi


def dot(a, b):
    return jnp.dot(a, b, preferred_element_type=F32)


def dot_nt(a, b):
    return lax.dot_general(a, b, (((1,), (1,)), ((), ())), preferred_element_type=F32)


def iota(shape, axis):
    return lax.broadcasted_iota(jnp.int32, shape, axis)


def ones_where(mask):
    return jnp.where(mask, 1.0, 0.0).astype(BF16)


def step_kernel(
    sizes,
    spec_hbm,
    state_hbm,
    win_ref,
    bias_ref,
    wout_ref,
    leg_hbm,
    rows_ref,
    modes_ref,
    spec_grad_ref,
    gin_ref,
    gbias_ref,
    gout_ref,
    spec_v,
    state_v,
    leg_v,
    legp,
    spec_pad,
    coef,
    win_ext,
    win_t,
    wout_t,
    table,
    scale_v,
    columns,
    factor,
    active,
    lhs,
    grid_cot,
    dstate,
    zbuf,
    out_acc,
    send1,
    recv1,
    send2,
    recv2,
    acc,
    part,
    pieces,
    zpieces,
    result,
    load_sem,
    a2a_send,
    a2a_recv,
    sum_send,
    sum_recv,
    ready,
):
    n, rows, chans, pad, lon, hid = sizes
    per = rows // CHUNKS
    group = per * n
    total = rows * n
    lines = n // PLANE
    me = lax.axis_index("wide")
    core = lax.axis_index("dp")
    line, spot = lax.div(me, PLANE), lax.rem(me, PLANE)
    line_at = [lax.rem(line + t, lines) * PLANE for t in range(lines)]

    def spot_at(t):
        return lax.rem(spot + t, PLANE)

    leg_copy = pltpu.make_async_copy(leg_hbm, leg_v, load_sem.at[0])
    spec_copy = pltpu.make_async_copy(spec_hbm, spec_v, load_sem.at[1])
    state_copy = pltpu.make_async_copy(state_hbm, state_v, load_sem.at[2])
    leg_copy.start()
    spec_copy.start()
    state_copy.start()

    barrier = pltpu.get_barrier_semaphore()
    for t in range(1, lines):
        pl.semaphore_signal(
            barrier, inc=1, device_id={"wide": line_at[t] + spot}, device_id_type=MESH
        )
    for t in range(1, PLANE):
        pl.semaphore_signal(
            barrier, inc=1, device_id={"wide": line_at[0] + spot_at(t)}, device_id_type=MESH
        )
    for t in range(PLANE):
        pl.semaphore_signal(
            barrier,
            inc=1,
            device_id={"dp": 1 - core, "wide": line_at[0] + spot_at(t)},
            device_id_type=MESH,
        )

    def chunked(at):
        ch = lax.div(at, group)
        inner = at - ch * group
        owner = lax.div(inner, per)
        return owner * rows + ch * per + (inner - owner * per)

    order = ones_where(iota((total, total), 0) == chunked(iota((total, total), 1)))
    row_at = rows_ref[...]
    north = jnp.minimum(row_at, total - 1 - row_at).astype(F32).astype(BF16)
    north = dot(jnp.broadcast_to(north, (16, total)), order)
    weights = jnp.sin((north[0:8] + 0.5) * (math.pi / total)) * (math.pi / total)

    modes = modes_ref[...].astype(F32).astype(BF16)
    modes = jnp.broadcast_to(modes, (LANES, 2 * n))

    leg_copy.wait()
    for i in range(2):
        legp[i] = dot(leg_v[i], order).astype(BF16)
    spec_copy.wait()
    zero_rows = jnp.zeros((pad - chans, spec_v.shape[2]), F32)
    for i in range(2):
        both = spec_v[i].astype(F32)
        spec_pad[...] = jnp.concatenate(
            [both[0:chans], zero_rows, both[chans : 2 * chans], zero_rows], axis=0
        ).astype(BF16)
        got = dot(spec_pad[...], legp[i])
        coef[pl.ds(i * 2 * pad, 2 * pad), :] = (got * weights[0:1]).astype(BF16)

    def to_messages(flat):
        return flat.reshape(n, per, 4 * pad)

    for ch in range(CHUNKS):
        send1[ch] = to_messages(coef[:, pl.ds(ch * group, group)].T)
        recv1[ch, me] = send1[ch, me]

    pl.semaphore_wait(barrier, lines - 1 + 2 * PLANE - 1)
    for t in range(1, PLANE):
        pl.semaphore_signal(
            ready, inc=1, device_id={"wide": line_at[0] + spot_at(t)}, device_id_type=MESH
        )
    pl.semaphore_wait(ready, PLANE - 1)

    def spread(src, dst, slot):
        def go(to):
            pltpu.make_async_remote_copy(
                src.at[to],
                dst.at[me],
                a2a_send.at[slot],
                a2a_recv.at[slot],
                device_id={"wide": to},
                device_id_type=MESH,
            ).start()

        for t in range(1, lines):
            go(line_at[t] + spot)

        @pl.loop(1, PLANE)
        def _(t):
            at = spot_at(t)
            for s in range(lines):
                go(line_at[s] + at)

    def spread_rest(src, dst, slot):
        return pltpu.make_async_remote_copy(
            src.at[pl.ds(0, n - 1)],
            dst.at[pl.ds(0, n - 1)],
            a2a_send.at[slot],
            a2a_recv.at[slot],
            device_id={"wide": line_at[1] + spot},
            device_id_type=MESH,
        )

    for ch in range(CHUNKS):
        spread(send1.at[ch], recv1.at[ch], ch)

    win_rows = win_ref[...].astype(F32)
    bias = bias_ref[...]
    bias_parts = []
    for _ in range(3):
        high = bias.astype(BF16).astype(F32)
        bias_parts.append(high)
        bias = bias - high
    rest_rows = jnp.zeros((pad - chans - 3, hid), F32)
    extended = jnp.concatenate([win_rows] + bias_parts + [rest_rows], axis=0)
    win_ext[...] = extended.astype(BF16)
    win_t[...] = extended.T.astype(BF16)
    wout_rows = jnp.concatenate(
        [wout_ref[...].astype(F32), jnp.zeros((pad - chans, hid), F32)], axis=0
    )
    wout_t[...] = wout_rows.T.astype(BF16)

    state_copy.wait()
    flat_state = state_v[...].reshape(chans * rows, lon)
    row_id = iota((pad, lon), 0)
    one_rows = jnp.logical_and(row_id >= chans, row_id < chans + 3)
    for j in range(rows):
        pick = ones_where(
            iota((pad, chans * rows), 1) == rows * iota((pad, chans * rows), 0) + j
        )
        columns[j] = jnp.where(one_rows, 1.0, dot(pick, flat_state)).astype(BF16)

    @pl.loop(0, rows)
    def _(j):
        preact = dot(win_t[...], columns[j])
        gate = jax.nn.sigmoid(preact)
        active[j] = (preact * gate).astype(BF16)
        factor[j] = gate * (1.0 + preact * (1.0 - gate))

    for i in range(2):
        choose = ones_where(iota((n, 2 * n), 1) == 2 * iota((n, 2 * n), 0) + i)
        mode = dot_nt(choose, modes)
        phase = mode * iota((n, LANES), 1).astype(F32)
        phase = phase - lon * jnp.floor(phase * (1.0 / lon))
        real, imag = jnp.cos(phase * (TURN / lon)), jnp.sin(phase * (TURN / lon))
        parts = lon // LANES
        jump = mode - parts * jnp.floor(mode * (1.0 / parts))
        jump_real, jump_imag = jnp.cos(jump * (TURN / parts)), jnp.sin(jump * (TURN / parts))
        for b in range(parts):
            at = pl.ds(b * LANES, LANES)
            table[pl.ds(2 * i * n, n), at] = real.astype(BF16)
            table[pl.ds((2 * i + 1) * n, n), at] = (-imag).astype(BF16)
            real, imag = real * jump_real - imag * jump_imag, imag * jump_real + real * jump_imag
    slot_modes = []
    for i in range(2):
        choose = ones_where(iota((2 * n, n), 0) == 2 * iota((2 * n, n), 1) + i)
        slot_modes += [dot(modes[0:16], choose)] * 2
    scale_v[...] = jnp.where(jnp.concatenate(slot_modes, axis=1) == 0.0, 1.0, 2.0)[0:8]

    def row_major(at):
        j = lax.div(at, n)
        return (at - j * n) * per + j

    regroup = ones_where(iota((group, group), 0) == row_major(iota((group, group), 1)))

    for ch in range(CHUNKS):
        spread_rest(send1.at[ch], recv1.at[ch], ch).wait_recv()
        arrived = recv1[ch].reshape(group, 4 * pad).T
        arrived = dot(arrived, regroup).astype(BF16)
        for j in range(per):
            for q in range(4):
                lhs[pl.ds(j * pad, pad), pl.ds(q * n, n)] = arrived[
                    q * pad : (q + 1) * pad, j * n : (j + 1) * n
                ]
        grid_cot[ch] = (dot(lhs[...], table[...]) * (1.0 / lon)).astype(BF16)
        for j in range(per):
            row = ch * per + j
            mine = pl.ds(j * pad, pad)
            cot_row = grid_cot[ch, mine, :]
            grad_preact = (dot(wout_t[...], cot_row) * factor[row]).astype(BF16)
            dstate[mine, :] = dot(win_ext[...], grad_preact).astype(BF16)
            grad_in = dot_nt(columns[row], grad_preact)
            grad_out = dot_nt(cot_row, active[row])
            if row == 0:
                acc[0] = grad_in
                acc[1] = grad_out
            else:
                acc[0] += grad_in
                acc[1] += grad_out
        back = (dot_nt(dstate[...], table[...]) * scale_v[0:1, :]).astype(BF16)
        for j in range(per):
            for q in range(4):
                zbuf[pl.ds(q * pad, pad), pl.ds(j * n, n)] = back[
                    j * pad : (j + 1) * pad, q * n : (q + 1) * n
                ]
        send2[ch] = to_messages(dot_nt(regroup, zbuf[...]).astype(BF16))
        recv2[ch, me] = send2[ch, me]
        spread(send2.at[ch], recv2.at[ch], CHUNKS + ch)

    share = 2 * pad // (2 * PLANE) // 2
    part[...] = acc[...].reshape(2, pad // 2, 2, hid)

    def piece(c, s):
        return part.at[c, pl.ds(s * share, share)]

    def meet(src, dst, slot, to):
        return pltpu.make_async_remote_copy(
            src,
            dst,
            sum_send.at[slot],
            sum_recv.at[slot],
            device_id=to,
            device_id_type=MESH,
        )

    mine = core * PLANE + spot
    pieces[mine] = part[core, pl.ds(spot * share, share)]
    for t in range(PLANE):
        for c in (1, 0):
            if t or c:
                owner = lax.rem(core + c, 2)
                at = spot_at(t)
                to = {"dp": owner, "wide": line_at[0] + at}
                meet(piece(owner, at), pieces.at[mine], 0, to).start()
    others = meet(
        pieces.at[pl.ds(0, 2 * PLANE - 1)],
        pieces.at[pl.ds(0, 2 * PLANE - 1)],
        0,
        {"dp": 1 - core, "wide": me},
    )
    others.wait_recv()
    others.wait_send()
    summed = pieces[0]
    for t in range(1, 2 * PLANE):
        summed = summed + pieces[t]
    zpieces[line] = summed
    for t in range(1, lines):
        meet(zpieces.at[line], zpieces.at[line], 1, {"wide": line_at[t] + spot}).start()
    others = meet(
        zpieces.at[pl.ds(0, lines - 1)],
        zpieces.at[pl.ds(0, lines - 1)],
        1,
        {"wide": line_at[1] + spot},
    )
    others.wait_recv()
    others.wait_send()
    summed = zpieces[0]
    for t in range(1, lines):
        summed = summed + zpieces[t]
    result[mine] = summed
    for t in range(PLANE):
        for c in (1, 0):
            if t or c:
                owner = lax.rem(core + c, 2)
                to = {"dp": owner, "wide": line_at[0] + spot_at(t)}
                meet(result.at[mine], result.at[mine], 2, to).start()

    for ch in range(CHUNKS):
        spread_rest(send2.at[ch], recv2.at[ch], CHUNKS + ch).wait_recv()
        arrived = recv2[ch].reshape(group, 4 * pad).T
        for i in range(2):
            got = dot_nt(
                arrived[2 * i * pad : 2 * (i + 1) * pad], legp[i, :, pl.ds(ch * group, group)]
            )
            if ch:
                got = got + out_acc[i]
            if ch < CHUNKS - 1:
                out_acc[i] = got
            else:
                spec_grad_ref[i] = jnp.concatenate(
                    [got[0:chans], got[pad : pad + chans]], axis=0
                ).astype(BF16)

    others = meet(
        result.at[pl.ds(0, 2 * PLANE - 1)],
        result.at[pl.ds(0, 2 * PLANE - 1)],
        2,
        {"dp": 1 - core, "wide": me},
    )
    others.wait_recv()
    others.wait_send()
    grad_in = result[pl.ds(0, PLANE)].reshape(pad, hid)
    gin_ref[...] = grad_in[0:chans]
    gbias_ref[...] = grad_in[chans : chans + 1]
    gout_ref[...] = result[pl.ds(PLANE, PLANE)].reshape(pad, hid)[0:chans]
    for ch in range(CHUNKS):
        spread_rest(send1.at[ch], recv1.at[ch], ch).wait_send()
        spread_rest(send2.at[ch], recv2.at[ch], CHUNKS + ch).wait_send()


def settle_kernel(*refs):
    count = (len(refs) - 2) // 3
    loads, stores = [], []
    for i in range(count):
        held = refs[2 * count + i]
        loads.append(pltpu.make_async_copy(refs[i], held, refs[-2].at[i]))
        stores.append(pltpu.make_async_copy(held, refs[count + i], refs[-1].at[i]))
        loads[i].start()
    for i in range(count):
        loads[i].wait()
        stores[i].start()
    for i in range(count):
        stores[i].wait()


def settle(*arrays):
    anywhere = pl.BlockSpec(memory_space=pl.ANY)
    sems = pltpu.SemaphoreType.DMA((len(arrays),))
    return pl.pallas_call(
        settle_kernel,
        name="settle",
        out_shape=[jax.ShapeDtypeStruct(x.shape, x.dtype) for x in arrays],
        in_specs=[anywhere] * len(arrays),
        out_specs=[anywhere] * len(arrays),
        scratch_shapes=[pltpu.VMEM(x.shape, x.dtype) for x in arrays] + [sems, sems],
        compiler_params=pltpu.CompilerParams(vmem_limit_bytes=56 * 2**20),
    )(*arrays)


def per_device(
    spec_cot, grid_state, weight_in, bias_in, weight_out, legendre, row_order, mode_order
):
    n = lax.axis_size("wide")
    _, rows, lon, chans = grid_state.shape
    hid = weight_in.shape[1]
    degrees = legendre.shape[1]
    pad = -(-(chans + 3) // 32) * 32
    total, group = rows * n, rows * n // CHUNKS
    per = rows // CHUNKS
    share = pad // PLANE // 2
    message = (CHUNKS, n, per, 4 * pad)
    scratch = [
        pltpu.VMEM((2, 2 * chans, degrees), BF16),
        pltpu.VMEM((chans, rows, lon), BF16),
        pltpu.VMEM((2, degrees, total), BF16),
        pltpu.VMEM((2, degrees, total), BF16),
        pltpu.VMEM((2 * pad, degrees), BF16),
        pltpu.VMEM((4 * pad, total), BF16),
        pltpu.VMEM((pad, hid), BF16),
        pltpu.VMEM((hid, pad), BF16),
        pltpu.VMEM((hid, pad), BF16),
        pltpu.VMEM((4 * n, lon), BF16),
        pltpu.VMEM((8, 4 * n), F32),
        pltpu.VMEM((rows, pad, lon), BF16),
        pltpu.VMEM((rows, hid, lon), F32),
        pltpu.VMEM((rows, hid, lon), BF16),
        pltpu.VMEM((per * pad, 4 * n), BF16),
        pltpu.VMEM((CHUNKS, per * pad, lon), BF16),
        pltpu.VMEM((per * pad, lon), BF16),
        pltpu.VMEM((4 * pad, group), BF16),
        pltpu.VMEM((2, 2 * pad, degrees), F32),
        pltpu.VMEM(message, BF16),
        pltpu.VMEM(message, BF16),
        pltpu.VMEM(message, BF16),
        pltpu.VMEM(message, BF16),
        pltpu.VMEM((2, pad, hid), F32),
        pltpu.VMEM((2, pad // 2, 2, hid), F32),
        pltpu.VMEM((2 * PLANE, share, 2, hid), F32),
        pltpu.VMEM((n // PLANE, share, 2, hid), F32),
        pltpu.VMEM((2 * PLANE, share, 2, hid), F32),
        pltpu.SemaphoreType.DMA((3,)),
        pltpu.SemaphoreType.DMA((2 * CHUNKS,)),
        pltpu.SemaphoreType.DMA((2 * CHUNKS,)),
        pltpu.SemaphoreType.DMA((3,)),
        pltpu.SemaphoreType.DMA((3,)),
        pltpu.SemaphoreType.REGULAR,
    ]
    vmem = pl.BlockSpec(memory_space=pltpu.VMEM)
    hbm = pl.BlockSpec(memory_space=pl.ANY)
    spec_grad, grad_in, grad_bias, grad_out = pl.pallas_call(
        functools.partial(step_kernel, (n, rows, chans, pad, lon, hid)),
        name="spectral_step",
        out_shape=(
            jax.ShapeDtypeStruct((2, 2 * chans, degrees), BF16),
            jax.ShapeDtypeStruct((chans, hid), F32),
            jax.ShapeDtypeStruct((1, hid), F32),
            jax.ShapeDtypeStruct((chans, hid), F32),
        ),
        in_specs=[hbm, hbm, vmem, vmem, vmem, hbm, vmem, vmem],
        out_specs=(vmem, vmem, vmem, vmem),
        scratch_shapes=scratch,
        compiler_params=pltpu.CompilerParams(
            collective_id=0, has_side_effects=True, vmem_limit_bytes=56 * 2**20
        ),
    )(
        jnp.swapaxes(spec_cot[0], 1, 2),
        jnp.transpose(grid_state[0], (2, 0, 1)),
        weight_in,
        bias_in.reshape(1, hid),
        weight_out.T,
        legendre,
        row_order.reshape(1, total),
        mode_order.reshape(1, 2 * n),
    )
    spec_grad, grad_in, grad_bias, grad_out = settle(spec_grad, grad_in, grad_bias, grad_out)
    return (
        jnp.swapaxes(spec_grad, 1, 2)[None],
        grad_in,
        grad_bias.reshape(hid),
        grad_out.T,
    )


def solution(mesh):
    placed = (
        P("dp", "wide", None, None),
        P("dp", "wide", None, None),
        P(),
        P(),
        P(),
        P("wide", None, None),
        P(),
        P(),
    )
    return jax.shard_map(
        per_device,
        mesh=mesh,
        in_specs=placed,
        out_specs=(P("dp", "wide", None, None), P(), P(), P()),
        check_vma=False,
    )
```

time: 345 us -> 59.6 us (0.17)
  waiting for transfers between devices: 176 us -> 0 us
  blocking collectives: 78.1 us -> 0 us
  Pallas kernels: 0 us -> 58.8 us
  starting transfers between devices: 24.1 us -> 0 us
  local copies, waits for them, and re-layouts: 20.2 us -> 0 us
  matrix products: 19.8 us -> 0 us
  between operations: 14.2 us -> 0.64 us
  other arithmetic: 11.9 us -> 0 us
    psum x1 -> x0, waiting for transfers between devices: 169 us -> none  [per_device(): lax.psum((local_in, local_bias, local_out), ('dp', 'wide'))]
    psum x1 -> x0, blocking collectives: 78.1 us -> none  [per_device(): lax.psum((local_in, local_bias, local_out), ('dp', 'wide'))]
    pallas_call x0 -> x2, Pallas kernels: none -> 58.8 us  [the longest x1 57 us: per_device(): pl.pallas_call(functools.partial(step_kernel, (n, rows, chans, pad, lon,...]
    all_to_all x2 -> x0, starting transfers between devices: 24.1 us -> none  [the longest x1 16.5 us: per_device(): lax.all_to_all(fourier_cot, 'wide', split_axis=1, concat_axis=2, tiled=True)]
    dot_general x9 -> x0, matrix products: 19.8 us -> none  [the longest x1 4.24 us: per_device(): jnp.einsum('rh,rc->hc', activation, cot_rows, preferred_element_type=jnp....]
    another operation x2 -> x0, other arithmetic: 11.1 us -> none
    unnamed x24 -> x0, local copies, waits for them, and re-layouts: 9.65 us -> none
    all_to_all x2 -> x0, waiting for transfers between devices: 7.23 us -> none  [the longest x1 7.23 us: per_device(): lax.all_to_all(fourier_cot, 'wide', split_axis=1, concat_axis=2, tiled=True)]
  transfers between devices with their start and end apart: 3 -> 0, of which waited for: 2 -> 0; matrix products, arithmetic and copies ran while one was open for 7% -> 0% of each run, Pallas kernels for 0% -> 0%
where the time goes in v3:
time: 59.6 us; the launch traced here: 59.5 us
  Pallas kernels  58.8 us (99%)
  between operations  0.64 us (1%)
    pallas_call x1, Pallas kernels, per_device(): pl.pallas_call(functools.partial(step_kernel, (n, rows, chans, pad, lon,...  57 us
    pallas_call x1, Pallas kernels, settle(): pl.pallas_call(settle_kernel, name='settle', out_shape=[jax.ShapeDtypeStr...  1.85 us

profile of v3, /device:TPU:1, one launch (start us, length us, event | category | flops | bytes accessed | tf_op | source)
XLA Modules:
  0.0 59.5 jit_solution(15138749250188319558)
XLA Ops:
  0.6 57.0 %spectral_step.1 = (bf16[2,296,256]{2,1,0:T(8,128)(2,1)}, f32[148,256]{1,0:T(8,128)}, f32[1,256]{1,0:T(1,128)}, f32[148,256]{1,0:T(8,128)}) custom-call(bf16[2,296,256]{2,1,0:T(8,128)(2,1)} %bitcast.16, bf16[148,4,1024]{2,1,0:T(4,128)(2,1)} %bitcast.15, bf16[148,256]{1,0:T(8,128)(2,1)} %win_ref.1, f32[1,256]{1,0:T(1,128)} %bitcast.19, ...), custom_call_target="tpu_custom_call" | custom-call | tf_op jit(solution)/shard_map/spectral_step/pallas_call | solution.py:460
  57.6 1.9 %settle.1 = (bf16[2,296,256]{2,1,0:T(8,128)(2,1)}, f32[148,256]{1,0:T(8,128)}, f32[1,256]{1,0:T(1,128)}, f32[148,256]{1,0:T(8,128)}) custom-call(bf16[2,296,256]{2,1,0:T(8,128)(2,1)} %get-tuple-element.12.refs_0_, f32[148,256]{1,0:T(8,128)} %get-tuple-element.13.refs_1_, f32[1,256]{1,0:T(1,128)} %get-tuple-element.14.refs_2_, ...), custom_call_target="tpu_custom_call" | custom-call | tf_op jit(solution)/shard_map/settle/pallas_call | solution.py:399

commit v4 on v3

--- a/solution.py
+++ b/solution.py
@@ -37,19 +37,24 @@
     sizes,
     spec_hbm,
     state_hbm,
-    win_ref,
-    bias_ref,
-    wout_ref,
+    win_hbm,
+    bias_hbm,
+    wout_hbm,
     leg_hbm,
-    rows_ref,
-    modes_ref,
+    rows_hbm,
+    modes_hbm,
     spec_grad_ref,
     gin_ref,
     gbias_ref,
     gout_ref,
     spec_v,
     state_v,
+    win_ref,
+    bias_ref,
+    wout_ref,
     leg_v,
+    rows_ref,
+    modes_ref,
     legp,
     spec_pad,
     coef,
@@ -63,6 +68,7 @@
     active,
     lhs,
     grid_cot,
+    grad_hidden,
     dstate,
     zbuf,
     out_acc,
@@ -95,12 +101,24 @@
     def spot_at(t):
         return lax.rem(spot + t, PLANE)
 
-    leg_copy = pltpu.make_async_copy(leg_hbm, leg_v, load_sem.at[0])
-    spec_copy = pltpu.make_async_copy(spec_hbm, spec_v, load_sem.at[1])
-    state_copy = pltpu.make_async_copy(state_hbm, state_v, load_sem.at[2])
-    leg_copy.start()
-    spec_copy.start()
-    state_copy.start()
+    loads = [
+        pltpu.make_async_copy(src, dst, load_sem.at[at])
+        for at, (src, dst) in enumerate(
+            [
+                (leg_hbm, leg_v),
+                (rows_hbm, rows_ref),
+                (spec_hbm, spec_v),
+                (modes_hbm, modes_ref),
+                (state_hbm, state_v),
+                (win_hbm, win_ref),
+                (bias_hbm, bias_ref),
+                (wout_hbm, wout_ref),
+            ]
+        )
+    ]
+    for load in loads:
+        load.start()
+    leg_load, rows_load, spec_load, modes_load, state_load, *weight_loads = loads
 
     barrier = pltpu.get_barrier_semaphore()
     for t in range(1, lines):
@@ -111,13 +129,9 @@
         pl.semaphore_signal(
             barrier, inc=1, device_id={"wide": line_at[0] + spot_at(t)}, device_id_type=MESH
         )
-    for t in range(PLANE):
-        pl.semaphore_signal(
-            barrier,
-            inc=1,
-            device_id={"dp": 1 - core, "wide": line_at[0] + spot_at(t)},
-            device_id_type=MESH,
-        )
+    pl.semaphore_signal(
+        barrier, inc=1, device_id={"dp": 1 - core, "wide": me}, device_id_type=MESH
+    )
 
     def chunked(at):
         ch = lax.div(at, group)
@@ -125,43 +139,34 @@
         owner = lax.div(inner, per)
         return owner * rows + ch * per + (inner - owner * per)
 
-    order = ones_where(iota((total, total), 0) == chunked(iota((total, total), 1)))
+    order = ones_where(iota((total, total), 0) == chunked(iota((1, total), 1)))
+    leg_load.wait()
+    for i in range(2):
+        legp[i] = dot(leg_v[i], order).astype(BF16)
+
+    pl.semaphore_wait(barrier, lines + PLANE - 1)
+    for t in range(1, PLANE):
+        pl.semaphore_signal(
+            ready, inc=1, device_id={"wide": line_at[0] + spot_at(t)}, device_id_type=MESH
+        )
+
+    rows_load.wait()
     row_at = rows_ref[...]
     north = jnp.minimum(row_at, total - 1 - row_at).astype(F32).astype(BF16)
     north = dot(jnp.broadcast_to(north, (16, total)), order)
     weights = jnp.sin((north[0:8] + 0.5) * (math.pi / total)) * (math.pi / total)
-
-    modes = modes_ref[...].astype(F32).astype(BF16)
-    modes = jnp.broadcast_to(modes, (LANES, 2 * n))
-
-    leg_copy.wait()
-    for i in range(2):
-        legp[i] = dot(leg_v[i], order).astype(BF16)
-    spec_copy.wait()
+    spec_load.wait()
     zero_rows = jnp.zeros((pad - chans, spec_v.shape[2]), F32)
     for i in range(2):
         both = spec_v[i].astype(F32)
-        spec_pad[...] = jnp.concatenate(
+        spec_pad[i] = jnp.concatenate(
             [both[0:chans], zero_rows, both[chans : 2 * chans], zero_rows], axis=0
         ).astype(BF16)
-        got = dot(spec_pad[...], legp[i])
-        coef[pl.ds(i * 2 * pad, 2 * pad), :] = (got * weights[0:1]).astype(BF16)
 
     def to_messages(flat):
         return flat.reshape(n, per, 4 * pad)
 
-    for ch in range(CHUNKS):
-        send1[ch] = to_messages(coef[:, pl.ds(ch * group, group)].T)
-        recv1[ch, me] = send1[ch, me]
-
-    pl.semaphore_wait(barrier, lines - 1 + 2 * PLANE - 1)
-    for t in range(1, PLANE):
-        pl.semaphore_signal(
-            ready, inc=1, device_id={"wide": line_at[0] + spot_at(t)}, device_id_type=MESH
-        )
-    pl.semaphore_wait(ready, PLANE - 1)
-
-    def spread(src, dst, slot):
+    def spread(src, dst, slot, first=1, last=PLANE):
         def go(to):
             pltpu.make_async_remote_copy(
                 src.at[to],
@@ -172,10 +177,11 @@
                 device_id_type=MESH,
             ).start()
 
-        for t in range(1, lines):
-            go(line_at[t] + spot)
-
-        @pl.loop(1, PLANE)
+        if first == 1:
+            for t in range(1, lines):
+                go(line_at[t] + spot)
+
+        @pl.loop(first, last)
         def _(t):
             at = spot_at(t)
             for s in range(lines):
@@ -192,8 +198,20 @@
         )
 
     for ch in range(CHUNKS):
+        at = pl.ds(ch * group, group)
+        for i in range(2):
+            got = dot(spec_pad[i], legp[i, :, at])
+            coef[pl.ds(i * 2 * pad, 2 * pad), :] = (
+                got * weights[0:1, ch * group : (ch + 1) * group]
+            ).astype(BF16)
+        send1[ch] = to_messages(coef[...].T)
+        recv1[ch, me] = send1[ch, me]
+        if ch == 0:
+            pl.semaphore_wait(ready, PLANE - 1)
         spread(send1.at[ch], recv1.at[ch], ch)
 
+    for load in weight_loads:
+        load.wait()
     win_rows = win_ref[...].astype(F32)
     bias = bias_ref[...]
     bias_parts = []
@@ -210,7 +228,7 @@
     )
     wout_t[...] = wout_rows.T.astype(BF16)
 
-    state_copy.wait()
+    state_load.wait()
     flat_state = state_v[...].reshape(chans * rows, lon)
     row_id = iota((pad, lon), 0)
     one_rows = jnp.logical_and(row_id >= chans, row_id < chans + 3)
@@ -227,6 +245,9 @@
         active[j] = (preact * gate).astype(BF16)
         factor[j] = gate * (1.0 + preact * (1.0 - gate))
 
+    modes_load.wait()
+    modes = modes_ref[...].astype(F32).astype(BF16)
+    modes = jnp.broadcast_to(modes, (LANES, 2 * n))
     for i in range(2):
         choose = ones_where(iota((n, 2 * n), 1) == 2 * iota((n, 2 * n), 0) + i)
         mode = dot_nt(choose, modes)
@@ -251,7 +272,65 @@
         j = lax.div(at, n)
         return (at - j * n) * per + j
 
-    regroup = ones_where(iota((group, group), 0) == row_major(iota((group, group), 1)))
+    regroup = ones_where(iota((group, group), 0) == row_major(iota((1, group), 1)))
+
+    share = pad // PLANE // 2
+    own_piece = core * PLANE + spot
+
+    def meet(src, dst, slot, to):
+        return pltpu.make_async_remote_copy(
+            src,
+            dst,
+            sum_send.at[slot],
+            sum_recv.at[slot],
+            device_id=to,
+            device_id_type=MESH,
+        )
+
+    def meet_rest(buffer, slot):
+        count = buffer.shape[0] - 1
+        rest = buffer.at[pl.ds(0, count)]
+        return meet(rest, rest, slot, {"dp": 1 - core, "wide": me})
+
+    def over_plane(source, target, slot, owners):
+        for t in range(PLANE):
+            for c in owners:
+                at = spot_at(t)
+                to = {"dp": c, "wide": line_at[0] + at}
+
+                def go():
+                    meet(source(c, at), target.at[own_piece], slot, to).start()
+
+                if t:
+                    go()
+                else:
+                    pl.when(core != c)(go)
+
+    def sum_start(c):
+        part[c] = acc[c].reshape(pad // 2, 2, hid)
+
+        @pl.when(core == c)
+        def _():
+            pieces[own_piece] = part[c, pl.ds(spot * share, share)]
+
+        over_plane(lambda c, s: part.at[c, pl.ds(s * share, share)], pieces, 0, (c,))
+
+    def sum_middle():
+        meet_rest(pieces, 0).wait_recv()
+        summed = pieces[0]
+        for t in range(1, 2 * PLANE):
+            summed = summed + pieces[t]
+        zpieces[line] = summed
+        for t in range(1, lines):
+            meet(zpieces.at[line], zpieces.at[line], 1, {"wide": line_at[t] + spot}).start()
+
+    def sum_end():
+        meet_rest(zpieces, 1).wait_recv()
+        summed = zpieces[0]
+        for t in range(1, lines):
+            summed = summed + zpieces[t]
+        result[own_piece] = summed.astype(BF16)
+        over_plane(lambda c, s: result.at[own_piece], result, 2, (0, 1))
 
     for ch in range(CHUNKS):
         spread_rest(send1.at[ch], recv1.at[ch], ch).wait_recv()
@@ -265,18 +344,21 @@
         grid_cot[ch] = (dot(lhs[...], table[...]) * (1.0 / lon)).astype(BF16)
         for j in range(per):
             row = ch * per + j
+            grad = dot_nt(grid_cot[ch, pl.ds(j * pad, pad), :], active[row])
+            acc[1] = grad if row == 0 else acc[1] + grad
+        if ch == CHUNKS - 1:
+            sum_start(1)
+        for j in range(per):
+            row = ch * per + j
             mine = pl.ds(j * pad, pad)
-            cot_row = grid_cot[ch, mine, :]
-            grad_preact = (dot(wout_t[...], cot_row) * factor[row]).astype(BF16)
-            dstate[mine, :] = dot(win_ext[...], grad_preact).astype(BF16)
-            grad_in = dot_nt(columns[row], grad_preact)
-            grad_out = dot_nt(cot_row, active[row])
-            if row == 0:
-                acc[0] = grad_in
-                acc[1] = grad_out
-            else:
-                acc[0] += grad_in
-                acc[1] += grad_out
+            grad_preact = (dot(wout_t[...], grid_cot[ch, mine, :]) * factor[row]).astype(BF16)
+            grad_hidden[j] = grad_preact
+            grad = dot_nt(columns[row], grad_preact)
+            acc[0] = grad if row == 0 else acc[0] + grad
+        if ch == CHUNKS - 1:
+            sum_start(0)
+        for j in range(per):
+            dstate[pl.ds(j * pad, pad), :] = dot(win_ext[...], grad_hidden[j]).astype(BF16)
         back = (dot_nt(dstate[...], table[...]) * scale_v[0:1, :]).astype(BF16)
         for j in range(per):
             for q in range(4):
@@ -285,65 +367,12 @@
                 ]
         send2[ch] = to_messages(dot_nt(regroup, zbuf[...]).astype(BF16))
         recv2[ch, me] = send2[ch, me]
-        spread(send2.at[ch], recv2.at[ch], CHUNKS + ch)
-
-    share = 2 * pad // (2 * PLANE) // 2
-    part[...] = acc[...].reshape(2, pad // 2, 2, hid)
-
-    def piece(c, s):
-        return part.at[c, pl.ds(s * share, share)]
-
-    def meet(src, dst, slot, to):
-        return pltpu.make_async_remote_copy(
-            src,
-            dst,
-            sum_send.at[slot],
-            sum_recv.at[slot],
-            device_id=to,
-            device_id_type=MESH,
-        )
-
-    mine = core * PLANE + spot
-    pieces[mine] = part[core, pl.ds(spot * share, share)]
-    for t in range(PLANE):
-        for c in (1, 0):
-            if t or c:
-                owner = lax.rem(core + c, 2)
-                at = spot_at(t)
-                to = {"dp": owner, "wide": line_at[0] + at}
-                meet(piece(owner, at), pieces.at[mine], 0, to).start()
-    others = meet(
-        pieces.at[pl.ds(0, 2 * PLANE - 1)],
-        pieces.at[pl.ds(0, 2 * PLANE - 1)],
-        0,
-        {"dp": 1 - core, "wide": me},
-    )
-    others.wait_recv()
-    others.wait_send()
-    summed = pieces[0]
-    for t in range(1, 2 * PLANE):
-        summed = summed + pieces[t]
-    zpieces[line] = summed
-    for t in range(1, lines):
-        meet(zpieces.at[line], zpieces.at[line], 1, {"wide": line_at[t] + spot}).start()
-    others = meet(
-        zpieces.at[pl.ds(0, lines - 1)],
-        zpieces.at[pl.ds(0, lines - 1)],
-        1,
-        {"wide": line_at[1] + spot},
-    )
-    others.wait_recv()
-    others.wait_send()
-    summed = zpieces[0]
-    for t in range(1, lines):
-        summed = summed + zpieces[t]
-    result[mine] = summed
-    for t in range(PLANE):
-        for c in (1, 0):
-            if t or c:
-                owner = lax.rem(core + c, 2)
-                to = {"dp": owner, "wide": line_at[0] + spot_at(t)}
-                meet(result.at[mine], result.at[mine], 2, to).start()
+        if ch < CHUNKS - 1:
+            spread(send2.at[ch], recv2.at[ch], CHUNKS + ch, 1, 16)
+        else:
+            spread(send2.at[ch], recv2.at[ch], CHUNKS + ch)
+            sum_middle()
+            sum_end()
 
     for ch in range(CHUNKS):
         spread_rest(send2.at[ch], recv2.at[ch], CHUNKS + ch).wait_recv()
@@ -361,21 +390,17 @@
                     [got[0:chans], got[pad : pad + chans]], axis=0
                 ).astype(BF16)
 
-    others = meet(
-        result.at[pl.ds(0, 2 * PLANE - 1)],
-        result.at[pl.ds(0, 2 * PLANE - 1)],
-        2,
-        {"dp": 1 - core, "wide": me},
-    )
-    others.wait_recv()
-    others.wait_send()
-    grad_in = result[pl.ds(0, PLANE)].reshape(pad, hid)
+    meet_rest(result, 2).wait_recv()
+    grad_in = result[pl.ds(0, PLANE)].astype(F32).reshape(pad, hid)
     gin_ref[...] = grad_in[0:chans]
     gbias_ref[...] = grad_in[chans : chans + 1]
-    gout_ref[...] = result[pl.ds(PLANE, PLANE)].reshape(pad, hid)[0:chans]
+    gout_ref[...] = result[pl.ds(PLANE, PLANE)].astype(F32).reshape(pad, hid)[0:chans]
     for ch in range(CHUNKS):
         spread_rest(send1.at[ch], recv1.at[ch], ch).wait_send()
         spread_rest(send2.at[ch], recv2.at[ch], CHUNKS + ch).wait_send()
+    meet_rest(pieces, 0).wait_send()
+    meet_rest(zpieces, 1).wait_send()
+    meet_rest(result, 2).wait_send()
 
 
 def settle_kernel(*refs):
@@ -422,10 +447,15 @@
     scratch = [
         pltpu.VMEM((2, 2 * chans, degrees), BF16),
         pltpu.VMEM((chans, rows, lon), BF16),
+        pltpu.VMEM((chans, hid), BF16),
+        pltpu.VMEM((1, hid), F32),
+        pltpu.VMEM((chans, hid), BF16),
         pltpu.VMEM((2, degrees, total), BF16),
+        pltpu.VMEM((1, total), jnp.int32),
+        pltpu.VMEM((1, 2 * n), jnp.int32),
         pltpu.VMEM((2, degrees, total), BF16),
-        pltpu.VMEM((2 * pad, degrees), BF16),
-        pltpu.VMEM((4 * pad, total), BF16),
+        pltpu.VMEM((2, 2 * pad, degrees), BF16),
+        pltpu.VMEM((4 * pad, group), BF16),
         pltpu.VMEM((pad, hid), BF16),
         pltpu.VMEM((hid, pad), BF16),
         pltpu.VMEM((hid, pad), BF16),
@@ -436,6 +466,7 @@
         pltpu.VMEM((rows, hid, lon), BF16),
         pltpu.VMEM((per * pad, 4 * n), BF16),
         pltpu.VMEM((CHUNKS, per * pad, lon), BF16),
+        pltpu.VMEM((per, hid, lon), BF16),
         pltpu.VMEM((per * pad, lon), BF16),
         pltpu.VMEM((4 * pad, group), BF16),
         pltpu.VMEM((2, 2 * pad, degrees), F32),
@@ -447,8 +478,8 @@
         pltpu.VMEM((2, pad // 2, 2, hid), F32),
         pltpu.VMEM((2 * PLANE, share, 2, hid), F32),
         pltpu.VMEM((n // PLANE, share, 2, hid), F32),
-        pltpu.VMEM((2 * PLANE, share, 2, hid), F32),
-        pltpu.SemaphoreType.DMA((3,)),
+        pltpu.VMEM((2 * PLANE, share, 2, hid), BF16),
+        pltpu.SemaphoreType.DMA((8,)),
         pltpu.SemaphoreType.DMA((2 * CHUNKS,)),
         pltpu.SemaphoreType.DMA((2 * CHUNKS,)),
         pltpu.SemaphoreType.DMA((3,)),
@@ -466,7 +497,7 @@
             jax.ShapeDtypeStruct((1, hid), F32),
             jax.ShapeDtypeStruct((chans, hid), F32),
         ),
-        in_specs=[hbm, hbm, vmem, vmem, vmem, hbm, vmem, vmem],
+        in_specs=[hbm] * 8,
         out_specs=(vmem, vmem, vmem, vmem),
         scratch_shapes=scratch,
         compiler_params=pltpu.CompilerParams(

time: 59.6 us -> 56.7 us (0.951)
  Pallas kernels: 58.8 us -> 55.9 us
    pallas_call x1, Pallas kernels: 57 us -> 54 us  [per_device(): pl.pallas_call(functools.partial(step_kernel, (n, rows, chans, pad, lon,...]
where the time goes in v4:
time: 56.7 us; the launch traced here: 56.5 us
  Pallas kernels  55.9 us (99%)
  between operations  0.64 us (1%)
    pallas_call x1, Pallas kernels, per_device(): pl.pallas_call(functools.partial(step_kernel, (n, rows, chans, pad, lon,...  54 us
    pallas_call x1, Pallas kernels, settle(): pl.pallas_call(settle_kernel, name='settle', out_shape=[jax.ShapeDtypeStr...  1.85 us

profile of v4, /device:TPU:1, one launch (start us, length us, event | category | flops | bytes accessed | tf_op | source)
XLA Modules:
  0.0 56.5 jit_solution(8300632368957904575)
XLA Ops:
  0.6 54.0 %spectral_step.1 = (bf16[2,296,256]{2,1,0:T(8,128)(2,1)}, f32[148,256]{1,0:T(8,128)}, f32[1,256]{1,0:T(1,128)}, f32[148,256]{1,0:T(8,128)}) custom-call(bf16[2,296,256]{2,1,0:T(8,128)(2,1)} %bitcast.16, bf16[148,4,1024]{2,1,0:T(4,128)(2,1)} %bitcast.15, bf16[148,256]{1,0:T(8,128)(2,1)} %win_hbm.1, f32[1,256]{1,0:T(1,128)} %bitcast.19, ...), custom_call_target="tpu_custom_call" | custom-call | tf_op jit(solution)/shard_map/spectral_step/pallas_call | solution.py:491
  54.7 1.9 %settle.1 = (bf16[2,296,256]{2,1,0:T(8,128)(2,1)}, f32[148,256]{1,0:T(8,128)}, f32[1,256]{1,0:T(1,128)}, f32[148,256]{1,0:T(8,128)}) custom-call(bf16[2,296,256]{2,1,0:T(8,128)(2,1)} %get-tuple-element.12.refs_0_, f32[148,256]{1,0:T(8,128)} %get-tuple-element.13.refs_1_, f32[1,256]{1,0:T(1,128)} %get-tuple-element.14.refs_2_, ...), custom_call_target="tpu_custom_call" | custom-call | tf_op jit(solution)/shard_map/settle/pallas_call | solution.py:424

commit v5 on v4

--- a/solution.py
+++ b/solution.py
@@ -44,9 +44,8 @@
     rows_hbm,
     modes_hbm,
     spec_grad_ref,
-    gin_ref,
-    gbias_ref,
-    gout_ref,
+    sums_ref,
+    spec_out_v,
     spec_v,
     state_v,
     win_ref,
@@ -332,6 +331,18 @@
         result[own_piece] = summed.astype(BF16)
         over_plane(lambda c, s: result.at[own_piece], result, 2, (0, 1))
 
+    def gather_out(ch):
+        for j in range(per):
+            row = ch * per + j
+            grad = dot_nt(grid_cot[ch, pl.ds(j * pad, pad), :], active[row])
+            acc[1] = grad if row == 0 else acc[1] + grad
+
+    def gather_in(ch):
+        for j in range(per):
+            row = ch * per + j
+            grad = dot_nt(columns[row], grad_hidden[j])
+            acc[0] = grad if row == 0 else acc[0] + grad
+
     for ch in range(CHUNKS):
         spread_rest(send1.at[ch], recv1.at[ch], ch).wait_recv()
         arrived = recv1[ch].reshape(group, 4 * pad).T
@@ -342,20 +353,16 @@
                     q * pad : (q + 1) * pad, j * n : (j + 1) * n
                 ]
         grid_cot[ch] = (dot(lhs[...], table[...]) * (1.0 / lon)).astype(BF16)
-        for j in range(per):
-            row = ch * per + j
-            grad = dot_nt(grid_cot[ch, pl.ds(j * pad, pad), :], active[row])
-            acc[1] = grad if row == 0 else acc[1] + grad
-        if ch == CHUNKS - 1:
+        last = ch == CHUNKS - 1
+        if last:
+            gather_out(ch)
             sum_start(1)
         for j in range(per):
-            row = ch * per + j
-            mine = pl.ds(j * pad, pad)
-            grad_preact = (dot(wout_t[...], grid_cot[ch, mine, :]) * factor[row]).astype(BF16)
-            grad_hidden[j] = grad_preact
-            grad = dot_nt(columns[row], grad_preact)
-            acc[0] = grad if row == 0 else acc[0] + grad
-        if ch == CHUNKS - 1:
+            cot_row = grid_cot[ch, pl.ds(j * pad, pad), :]
+            back_hidden = dot(wout_t[...], cot_row)
+            grad_hidden[j] = (back_hidden * factor[ch * per + j]).astype(BF16)
+        if last:
+            gather_in(ch)
             sum_start(0)
         for j in range(per):
             dstate[pl.ds(j * pad, pad), :] = dot(win_ext[...], grad_hidden[j]).astype(BF16)
@@ -367,12 +374,13 @@
                 ]
         send2[ch] = to_messages(dot_nt(regroup, zbuf[...]).astype(BF16))
         recv2[ch, me] = send2[ch, me]
-        if ch < CHUNKS - 1:
-            spread(send2.at[ch], recv2.at[ch], CHUNKS + ch, 1, 16)
-        else:
-            spread(send2.at[ch], recv2.at[ch], CHUNKS + ch)
+        spread(send2.at[ch], recv2.at[ch], CHUNKS + ch)
+        if last:
             sum_middle()
             sum_end()
+        else:
+            gather_out(ch)
+            gather_in(ch)
 
     for ch in range(CHUNKS):
         spread_rest(send2.at[ch], recv2.at[ch], CHUNKS + ch).wait_recv()
@@ -386,50 +394,86 @@
             if ch < CHUNKS - 1:
                 out_acc[i] = got
             else:
-                spec_grad_ref[i] = jnp.concatenate(
+                spec_out_v[i] = jnp.concatenate(
                     [got[0:chans], got[pad : pad + chans]], axis=0
                 ).astype(BF16)
 
+    spec_out = pltpu.make_async_copy(spec_out_v, spec_grad_ref, load_sem.at[0])
+    spec_out.start()
     meet_rest(result, 2).wait_recv()
-    grad_in = result[pl.ds(0, PLANE)].astype(F32).reshape(pad, hid)
-    gin_ref[...] = grad_in[0:chans]
-    gbias_ref[...] = grad_in[chans : chans + 1]
-    gout_ref[...] = result[pl.ds(PLANE, PLANE)].astype(F32).reshape(pad, hid)[0:chans]
+    sums_out = pltpu.make_async_copy(result, sums_ref, load_sem.at[1])
+    sums_out.start()
     for ch in range(CHUNKS):
         spread_rest(send1.at[ch], recv1.at[ch], ch).wait_send()
         spread_rest(send2.at[ch], recv2.at[ch], CHUNKS + ch).wait_send()
     meet_rest(pieces, 0).wait_send()
     meet_rest(zpieces, 1).wait_send()
     meet_rest(result, 2).wait_send()
-
-
-def settle_kernel(*refs):
-    count = (len(refs) - 2) // 3
-    loads, stores = [], []
-    for i in range(count):
-        held = refs[2 * count + i]
-        loads.append(pltpu.make_async_copy(refs[i], held, refs[-2].at[i]))
-        stores.append(pltpu.make_async_copy(held, refs[count + i], refs[-1].at[i]))
-        loads[i].start()
-    for i in range(count):
-        loads[i].wait()
-        stores[i].start()
-    for i in range(count):
-        stores[i].wait()
-
-
-def settle(*arrays):
+    sums_out.wait()
+    spec_out.wait()
+
+
+def settle_kernel(
+    spec_hbm,
+    sums_hbm,
+    spec_out,
+    gin_out,
+    gbias_out,
+    gout_out,
+    spec_v,
+    sums_v,
+    gin_v,
+    gbias_v,
+    gout_v,
+    load_sem,
+    store_sem,
+):
+    chans, hid = gin_v.shape
+    spec_load = pltpu.make_async_copy(spec_hbm, spec_v, load_sem.at[0])
+    sums_load = pltpu.make_async_copy(sums_hbm, sums_v, load_sem.at[1])
+    stores = [
+        pltpu.make_async_copy(src, dst, store_sem.at[at])
+        for at, (src, dst) in enumerate(
+            [(spec_v, spec_out), (gin_v, gin_out), (gbias_v, gbias_out), (gout_v, gout_out)]
+        )
+    ]
+    sums_load.start()
+    spec_load.start()
+    half = sums_v.shape[0] // 2
+    pad = half * sums_v.shape[1] * 2
+    sums_load.wait()
+    grad_in = sums_v[pl.ds(0, half)].astype(F32).reshape(pad, hid)
+    gin_v[...] = grad_in[0:chans]
+    gbias_v[...] = grad_in[chans : chans + 1]
+    stores[1].start()
+    stores[2].start()
+    gout_v[...] = sums_v[pl.ds(half, half)].astype(F32).reshape(pad, hid)[0:chans]
+    stores[3].start()
+    spec_load.wait()
+    stores[0].start()
+    for store in stores:
+        store.wait()
+
+
+def settle(spec_grad, sums, chans, hid):
     anywhere = pl.BlockSpec(memory_space=pl.ANY)
-    sems = pltpu.SemaphoreType.DMA((len(arrays),))
+    shapes = [
+        jax.ShapeDtypeStruct(spec_grad.shape, spec_grad.dtype),
+        jax.ShapeDtypeStruct((chans, hid), F32),
+        jax.ShapeDtypeStruct((1, hid), F32),
+        jax.ShapeDtypeStruct((chans, hid), F32),
+    ]
+    held = [spec_grad, sums] + shapes[1:]
     return pl.pallas_call(
         settle_kernel,
         name="settle",
-        out_shape=[jax.ShapeDtypeStruct(x.shape, x.dtype) for x in arrays],
-        in_specs=[anywhere] * len(arrays),
-        out_specs=[anywhere] * len(arrays),
-        scratch_shapes=[pltpu.VMEM(x.shape, x.dtype) for x in arrays] + [sems, sems],
+        out_shape=shapes,
+        in_specs=[anywhere] * 2,
+        out_specs=[anywhere] * 4,
+        scratch_shapes=[pltpu.VMEM(x.shape, x.dtype) for x in held]
+        + [pltpu.SemaphoreType.DMA((2,)), pltpu.SemaphoreType.DMA((4,))],
         compiler_params=pltpu.CompilerParams(vmem_limit_bytes=56 * 2**20),
-    )(*arrays)
+    )(spec_grad, sums)
 
 
 def per_device(
@@ -445,6 +489,7 @@
     share = pad // PLANE // 2
     message = (CHUNKS, n, per, 4 * pad)
     scratch = [
+        pltpu.VMEM((2, 2 * chans, degrees), BF16),
         pltpu.VMEM((2, 2 * chans, degrees), BF16),
         pltpu.VMEM((chans, rows, lon), BF16),
         pltpu.VMEM((chans, hid), BF16),
@@ -486,19 +531,16 @@
         pltpu.SemaphoreType.DMA((3,)),
         pltpu.SemaphoreType.REGULAR,
     ]
-    vmem = pl.BlockSpec(memory_space=pltpu.VMEM)
     hbm = pl.BlockSpec(memory_space=pl.ANY)
-    spec_grad, grad_in, grad_bias, grad_out = pl.pallas_call(
+    spec_grad, sums = pl.pallas_call(
         functools.partial(step_kernel, (n, rows, chans, pad, lon, hid)),
         name="spectral_step",
         out_shape=(
             jax.ShapeDtypeStruct((2, 2 * chans, degrees), BF16),
-            jax.ShapeDtypeStruct((chans, hid), F32),
-            jax.ShapeDtypeStruct((1, hid), F32),
-            jax.ShapeDtypeStruct((chans, hid), F32),
+            jax.ShapeDtypeStruct((2 * PLANE, share, 2, hid), BF16),
         ),
         in_specs=[hbm] * 8,
-        out_specs=(vmem, vmem, vmem, vmem),
+        out_specs=(hbm, hbm),
         scratch_shapes=scratch,
         compiler_params=pltpu.CompilerParams(
             collective_id=0, has_side_effects=True, vmem_limit_bytes=56 * 2**20
@@ -513,7 +555,7 @@
         row_order.reshape(1, total),
         mode_order.reshape(1, 2 * n),
     )
-    spec_grad, grad_in, grad_bias, grad_out = settle(spec_grad, grad_in, grad_bias, grad_out)
+    spec_grad, grad_in, grad_bias, grad_out = settle(spec_grad, sums, chans, hid)
     return (
         jnp.swapaxes(spec_grad, 1, 2)[None],
         grad_in,

time: 56.7 us -> 56.3 us (level)
  no operation moved by 1% of the time
where the time goes in v5:
time: 56.3 us; the launch traced here: 56.2 us
  Pallas kernels  55.5 us (99%)
  between operations  0.64 us (1%)
    pallas_call x1, Pallas kernels, per_device(): pl.pallas_call(functools.partial(step_kernel, (n, rows, chans, pad, lon,...  53.7 us
    pallas_call x1, Pallas kernels, settle(): pl.pallas_call(settle_kernel, name='settle', out_shape=shapes, in_specs=[...  1.82 us

profile of v5, /device:TPU:1, one launch (start us, length us, event | category | flops | bytes accessed | tf_op | source)
XLA Modules:
  0.0 56.2 jit_solution(5392479446073651257)
XLA Ops:
  0.6 53.7 %spectral_step.1 = (bf16[2,296,256]{2,1,0:T(8,128)(2,1)}, bf16[32,5,2,256]{3,2,1,0:T(2,128)(2,1)}) custom-call(bf16[2,296,256]{2,1,0:T(8,128)(2,1)} %bitcast.16, bf16[148,4,1024]{2,1,0:T(4,128)(2,1)} %bitcast.15, bf16[148,256]{1,0:T(8,128)(2,1)} %win_hbm.1, f32[1,256]{1,0:T(1,128)} %bitcast.19, bf16[148,256]{1,0:T(8,128)(2,1)} %bitcast.17, ...), custom_call_target="tpu_custom_call" | custom-call | tf_op jit(solution)/shard_map/spectral_step/pallas_call | solution.py:535
  54.3 1.8 %settle.1 = (bf16[2,296,256]{2,1,0:T(8,128)(2,1)}, f32[148,256]{1,0:T(8,128)}, f32[1,256]{1,0:T(1,128)}, f32[148,256]{1,0:T(8,128)}) custom-call(bf16[2,296,256]{2,1,0:T(8,128)(2,1)} %get-tuple-element.10.spec_hbm, bf16[32,5,2,256]{3,2,1,0:T(2,128)(2,1)} %get-tuple-element.11.sums_hbm), custom_call_target="tpu_custom_call" | custom-call | tf_op jit(solution)/shard_map/settle/pallas_call | solution.py:467

commit v6 on v5

--- a/solution.py
+++ b/solution.py
@@ -132,17 +132,6 @@
         barrier, inc=1, device_id={"dp": 1 - core, "wide": me}, device_id_type=MESH
     )
 
-    def chunked(at):
-        ch = lax.div(at, group)
-        inner = at - ch * group
-        owner = lax.div(inner, per)
-        return owner * rows + ch * per + (inner - owner * per)
-
-    order = ones_where(iota((total, total), 0) == chunked(iota((1, total), 1)))
-    leg_load.wait()
-    for i in range(2):
-        legp[i] = dot(leg_v[i], order).astype(BF16)
-
     pl.semaphore_wait(barrier, lines + PLANE - 1)
     for t in range(1, PLANE):
         pl.semaphore_signal(
@@ -151,9 +140,8 @@
 
     rows_load.wait()
     row_at = rows_ref[...]
-    north = jnp.minimum(row_at, total - 1 - row_at).astype(F32).astype(BF16)
-    north = dot(jnp.broadcast_to(north, (16, total)), order)
-    weights = jnp.sin((north[0:8] + 0.5) * (math.pi / total)) * (math.pi / total)
+    north = jnp.minimum(row_at, total - 1 - row_at).astype(F32)
+    weights = jnp.sin((north + 0.5) * (math.pi / total)) * (math.pi / total)
     spec_load.wait()
     zero_rows = jnp.zeros((pad - chans, spec_v.shape[2]), F32)
     for i in range(2):
@@ -163,7 +151,7 @@
         ).astype(BF16)
 
     def to_messages(flat):
-        return flat.reshape(n, per, 4 * pad)
+        return flat.reshape(n, flat.shape[0] // n, 4 * pad)
 
     def spread(src, dst, slot, first=1, last=PLANE):
         def go(to):
@@ -196,18 +184,27 @@
             device_id_type=MESH,
         )
 
+    leg_load.wait()
+    for i in range(2):
+        got = dot(spec_pad[i], leg_v[i])
+        coef[pl.ds(i * 2 * pad, 2 * pad), :] = (got * weights).astype(BF16)
+    messages = to_messages(coef[...].T)
     for ch in range(CHUNKS):
-        at = pl.ds(ch * group, group)
-        for i in range(2):
-            got = dot(spec_pad[i], legp[i, :, at])
-            coef[pl.ds(i * 2 * pad, 2 * pad), :] = (
-                got * weights[0:1, ch * group : (ch + 1) * group]
-            ).astype(BF16)
-        send1[ch] = to_messages(coef[...].T)
+        send1[ch] = messages[:, ch * per : (ch + 1) * per]
         recv1[ch, me] = send1[ch, me]
-        if ch == 0:
-            pl.semaphore_wait(ready, PLANE - 1)
+    pl.semaphore_wait(ready, PLANE - 1)
+    for ch in range(CHUNKS):
         spread(send1.at[ch], recv1.at[ch], ch)
+
+    def chunked(at):
+        ch = lax.div(at, group)
+        inner = at - ch * group
+        owner = lax.div(inner, per)
+        return owner * rows + ch * per + (inner - owner * per)
+
+    order = ones_where(iota((total, total), 0) == chunked(iota((1, total), 1)))
+    for i in range(2):
+        legp[i] = dot(leg_v[i], order).astype(BF16)
 
     for load in weight_loads:
         load.wait()
@@ -500,7 +497,7 @@
         pltpu.VMEM((1, 2 * n), jnp.int32),
         pltpu.VMEM((2, degrees, total), BF16),
         pltpu.VMEM((2, 2 * pad, degrees), BF16),
-        pltpu.VMEM((4 * pad, group), BF16),
+        pltpu.VMEM((4 * pad, total), BF16),
         pltpu.VMEM((pad, hid), BF16),
         pltpu.VMEM((hid, pad), BF16),
         pltpu.VMEM((hid, pad), BF16),

time: 56.3 us -> 56.3 us (level)
  no operation moved by 1% of the time
where the time goes in v6:
time: 56.3 us; the launch traced here: 56.2 us
  Pallas kernels  55.5 us (99%)
  between operations  0.64 us (1%)
    pallas_call x1, Pallas kernels, per_device(): pl.pallas_call(functools.partial(step_kernel, (n, rows, chans, pad, lon,...  53.7 us
    pallas_call x1, Pallas kernels, settle(): pl.pallas_call(settle_kernel, name='settle', out_shape=shapes, in_specs=[...  1.82 us

profile of v6, /device:TPU:1, one launch (start us, length us, event | category | flops | bytes accessed | tf_op | source)
XLA Modules:
  0.0 56.2 jit_solution(11044312801239092872)
XLA Ops:
  0.6 53.7 %spectral_step.1 = (bf16[2,296,256]{2,1,0:T(8,128)(2,1)}, bf16[32,5,2,256]{3,2,1,0:T(2,128)(2,1)}) custom-call(bf16[2,296,256]{2,1,0:T(8,128)(2,1)} %bitcast.16, bf16[148,4,1024]{2,1,0:T(4,128)(2,1)} %bitcast.15, bf16[148,256]{1,0:T(8,128)(2,1)} %win_hbm.1, f32[1,256]{1,0:T(1,128)} %bitcast.19, bf16[148,256]{1,0:T(8,128)(2,1)} %bitcast.17, ...), custom_call_target="tpu_custom_call" | custom-call | tf_op jit(solution)/shard_map/spectral_step/pallas_call | solution.py:532
  54.3 1.8 %settle.1 = (bf16[2,296,256]{2,1,0:T(8,128)(2,1)}, f32[148,256]{1,0:T(8,128)}, f32[1,256]{1,0:T(1,128)}, f32[148,256]{1,0:T(8,128)}) custom-call(bf16[2,296,256]{2,1,0:T(8,128)(2,1)} %get-tuple-element.10.spec_hbm, bf16[32,5,2,256]{3,2,1,0:T(2,128)(2,1)} %get-tuple-element.11.sums_hbm), custom_call_target="tpu_custom_call" | custom-call | tf_op jit(solution)/shard_map/settle/pallas_call | solution.py:464
